TPU v7x, 32 devices: a whole 2x2x4 slice. The times are simulated.
32 devices in a mesh: fsdp: 8 (over z, core), mp: 4 (over y, x).
Axes of the slice: x: 2, y: 2, z: 4, core: 2. Of those that a mesh axis runs over, the one named last changes fastest.
Arguments:
- inputs: bfloat16 [2048, 2048], P('fsdp'), may hold values from -6 to 6
- cotangent: bfloat16 [2048, 2048], P('fsdp'), may hold values from -6 to 6
- lengths: int32 [2], replicated, may hold values from 256 to 1024, as said below
- attn_scale: float32 [2048], P('fsdp'), may hold values from 0.5 to 1.5
- w_query: float32 [2048, 2048], P('fsdp', 'mp'), may hold values from -0.015625 to 0.015625
- w_key: float32 [2048, 2048], P('fsdp', 'mp'), may hold values from -0.125 to 0.125
- w_value: float32 [2048, 2048], P('fsdp', 'mp'), may hold values from -0.125 to 0.125
- w_out: float32 [2048, 2048], P('mp', 'fsdp'), may hold values from -3 to 3
- rel_table: float32 [32, 32], P('fsdp', 'mp'), may hold values from -4 to 4
- ffn_scale: float32 [2048], P('fsdp'), may hold values from 0.5 to 1.5
- w_gate: float32 [2048, 5120], P('fsdp', 'mp'), may hold values from -0.125 to 0.125
- w_up: float32 [2048, 5120], P('fsdp', 'mp'), may hold values from -0.125 to 0.125
- w_down: float32 [5120, 2048], P('mp', 'fsdp'), may hold values from -0.078125 to 0.078125
Outputs:
- outputs: bfloat16 [2048, 2048], P('fsdp')
- d_inputs: bfloat16 [2048, 2048], P('fsdp')
- d_attn_scale: float32 [2048], P('fsdp')
- d_w_query: float32 [2048, 2048], P('fsdp', 'mp')
- d_w_key: float32 [2048, 2048], P('fsdp', 'mp')
- d_w_value: float32 [2048, 2048], P('fsdp', 'mp')
- d_w_out: float32 [2048, 2048], P('mp', 'fsdp')
- d_rel_table: float32 [32, 32], P('fsdp', 'mp')
- d_ffn_scale: float32 [2048], P('fsdp')
- d_w_gate: float32 [2048, 5120], P('fsdp', 'mp')
- d_w_up: float32 [2048, 5120], P('fsdp', 'mp')
- d_w_down: float32 [5120, 2048], P('mp', 'fsdp')
Inputs may be any that keep to these rules, and one draw needn't show every extreme that they name: lengths[s] slots at the start of sequence s are used, the rest is padding; in every draw some sequence is full.
All inputs are finite; a program needn't handle non-finite values.
Results may differ from a plain program's by a relative error of at most 0.019.
Values may be sent and summed in bfloat16 or wider, within the bound.
No kernel may reach another device: no remote copies, remote signals or barrier semaphores. Data moves between devices by JAX's collectives and lax.ppermute only.
A program may use at most 192 MiB of HBM per device.

v0:
```python
import functools

import jax
import jax.numpy as jnp
from jax import lax
from jax.experimental import pallas as pl
from jax.experimental.pallas import tpu as pltpu
from jax.sharding import Mesh, PartitionSpec as P

LOW = jnp.bfloat16
F32 = jnp.float32
CORES = 2
THRESHOLDS = (12, 16, 23, 32, 46, 64, 91)
EPSILON = 1e-06
MASKED = -1e30
SKEW = 128


def bucket_of(rel_offset):
    distance = jnp.abs(rel_offset)
    far_bucket = 8 + sum(((distance >= threshold).astype(jnp.int32) for threshold in THRESHOLDS))
    bucket_abs = jnp.where(distance < 8, distance, far_bucket)
    return bucket_abs + jnp.where(rel_offset > 0, 16, 0)


def bucket_onehot(buckets, seq_len):
    offset = lax.broadcasted_iota(jnp.int32, (buckets, 2 * seq_len), 1) - seq_len
    bucket = lax.broadcasted_iota(jnp.int32, (buckets, 2 * seq_len), 0)
    return bucket_of(offset) == bucket


def head_lanes(rows, width, head_width, head):
    lane = lax.broadcasted_iota(jnp.int32, (rows, width), 1)
    return (lane >= head * head_width) & (lane < (head + 1) * head_width)


def only(mask, values):
    return jnp.where(mask, values, jnp.zeros_like(values))


def block_place(block, core, near_count):
    return lax.rem(block, near_count) * CORES + lax.bitwise_xor(lax.div(block, near_count), core)


def bias_places(place_ref, step, blocks, rows, seq_len):
    core, near_count = place_ref[1], blocks // CORES
    query = block_place(step, core, near_count) * rows
    return [
        [
            pl.multiple_of(
                block_place(block, core, near_count) * rows - query - part * SKEW + seq_len - SKEW,
                SKEW,
            )
            for block in range(blocks)
        ]
        for part in range(rows // SKEW)
    ]


def forward_kernel(heads, shard, near_count, count, place_ref, *refs):
    own_ref, moved_ref, core_ref, core_moved_ref, got_ref, table_ref = refs[:6]
    qkv_ref, o_ref, p_ref = refs[6:9]
    other_refs, mine_refs = refs[9 : 9 + count], refs[9 + count : 9 + 2 * count]
    skew_ref, held_ref = refs[9 + 2 * count :]
    step = pl.program_id(0)
    seq_len = qkv_ref.shape[0]
    rows, width = o_ref.shape
    model = held_ref.shape[1]
    head_width = width // heads
    span = 2 * seq_len
    blocks = seq_len // rows
    block = row_block(step, near_count)

    @pl.when(step == 0)
    def _():
        weight = got_ref[:, :shard, : 3 * width].reshape(model, 3 * width)
        near = place_ref[4]
        for at, ref in enumerate((own_ref, moved_ref, core_ref, core_moved_ref)):
            first = (at // 2) * near_count + lax.bitwise_xor(near, at % 2)
            qkv_ref[pl.ds(pl.multiple_of(first * rows, rows), rows), :] = rows_dot(
                ref[...], weight
            ).astype(LOW)
        one_hot = bucket_onehot(table_ref.shape[0], seq_len)
        table = table_ref[...].astype(F32)
        column = lax.broadcasted_iota(jnp.int32, table.shape, 1)
        for head in range(heads):
            here = column == place_ref[2] * heads + head
            levels = jnp.sum(jnp.where(here, table, 0.0), axis=1, keepdims=True)
            line = jnp.sum(jnp.where(one_hot, levels, 0.0), axis=0, keepdims=True)
            line = jnp.broadcast_to(line, (SKEW, span))
            skew_ref[head] = pltpu.roll(line, span - SKEW, 1, stride=1, stride_axis=0)

    row = lax.broadcasted_iota(jnp.int32, (1, rows), 1)
    allowed = jnp.concatenate(
        [
            block_place(at, place_ref[1], near_count) * rows + row < place_ref[0]
            for at in range(blocks)
        ],
        1,
    )
    queries = qkv_ref[pl.ds(pl.multiple_of(block * rows, rows), rows), :width]
    keys = qkv_ref[:, width : 2 * width]
    values = qkv_ref[:, 2 * width :]
    total = jnp.zeros((rows, width), F32)
    places = bias_places(place_ref, block, blocks, rows, seq_len)
    for head in range(heads):
        scores = lax.dot_general(
            only(head_lanes(rows, width, head_width, head), queries),
            keys,
            (((1,), (1,)), ((), ())),
            preferred_element_type=F32,
        )
        bias = jnp.concatenate(
            [
                jnp.concatenate([skew_ref[head, :, pl.ds(place, rows)] for place in part], 1)
                for part in places
            ],
            0,
        )
        scores = jnp.where(allowed, scores + bias, MASKED)
        grown = jnp.exp(scores - jnp.max(scores, axis=1, keepdims=True))
        prob = (grown * (1.0 / jnp.sum(grown, axis=1, keepdims=True))).astype(LOW)
        p_ref[head] = prob
        total = total + jnp.dot(
            prob,
            only(head_lanes(seq_len, width, head_width, head), values),
            preferred_element_type=F32,
        )
    attended = total.astype(LOW)
    o_ref[...] = attended
    weight = got_ref[:, :shard, 3 * width :].reshape(model, width)
    held_ref[...] = contract_cols(attended, weight).astype(LOW)
    send_rows(step, near_count, place_ref[3], held_ref, other_refs, mine_refs)


def attention_forward(parts, got, table, place, heads, shard, count):
    rows, model = parts[0].shape
    blocks = len(parts)
    near_count = blocks // CORES
    seq_len, width = rows * blocks, got.shape[2] // 4
    out_specs, out_shape = sent_specs(near_count, count, rows // count, model)

    def fixed(shape):
        return pl.BlockSpec(shape, lambda i: (0,) * len(shape))

    outs = pl.pallas_call(
        functools.partial(forward_kernel, heads, shard, near_count, count),
        grid=(blocks,),
        in_specs=[pl.BlockSpec(memory_space=pltpu.SMEM)]
        + [fixed(part.shape) for part in parts]
        + [fixed(got.shape), fixed(table.shape)],
        out_specs=[
            fixed((seq_len, 3 * width)),
            pl.BlockSpec((rows, width), lambda i: (row_block(i, near_count), 0)),
            pl.BlockSpec((heads, rows, seq_len), lambda i: (0, row_block(i, near_count), 0)),
        ]
        + out_specs,
        out_shape=[
            jax.ShapeDtypeStruct((seq_len, 3 * width), LOW),
            jax.ShapeDtypeStruct((seq_len, width), LOW),
            jax.ShapeDtypeStruct((heads, seq_len, seq_len), LOW),
        ]
        + out_shape,
        scratch_shapes=[
            pltpu.VMEM((heads, SKEW, 2 * seq_len), F32),
            pltpu.VMEM((rows, model), LOW),
        ],
        compiler_params=pltpu.CompilerParams(vmem_limit_bytes=34 * 2**20),
        cost_estimate=pl.CostEstimate(flops=0, bytes_accessed=0, transcendentals=0),
        name="attention_forward",
    )(place, *parts, got, table)
    return (*outs[:3], outs[3 + count :], outs[3 : 3 + count])


def backward_kernel(heads, shard, near_count, count, place_ref, *refs):
    came, refs = refs[: 2 * count], refs[2 * count :]
    p_ref, got_ref, qkv_ref, d_ref, dt_ref, rows_ref, dk_sum, dv_sum, skew_ref = refs
    step = pl.program_id(0)
    block = row_block(step, near_count)
    take_rows(step, near_count, place_ref[3], came[:count], came[count:], rows_ref)
    rows, model = rows_ref.shape
    seq_len = qkv_ref.shape[0]
    width = qkv_ref.shape[1] // 3
    head_width = width // heads
    span = 2 * seq_len
    blocks = seq_len // rows

    @pl.when(step == 0)
    def _():
        dk_sum[...] = jnp.zeros_like(dk_sum)
        dv_sum[...] = jnp.zeros_like(dv_sum)
        skew_ref[...] = jnp.zeros_like(skew_ref)

    here = pl.ds(pl.multiple_of(block * rows, rows), rows)
    queries = qkv_ref[here, :width]
    keys = qkv_ref[:, width : 2 * width]
    values = qkv_ref[:, 2 * width :]
    weight = got_ref[:, :shard, 3 * width :].reshape(model, width)
    grads = rows_dot(rows_ref[...], weight).astype(LOW)
    total = jnp.zeros((rows, width), F32)
    places = bias_places(place_ref, block, blocks, rows, seq_len)
    for head in range(heads):
        own = head_lanes(rows, width, head_width, head)
        own_grads = only(own, grads)
        d_prob = lax.dot_general(
            own_grads, values, (((1,), (1,)), ((), ())), preferred_element_type=F32
        )
        prob_low = p_ref[head]
        prob = prob_low.astype(F32)
        weighed = prob * d_prob
        d_scores = (weighed - prob * jnp.sum(weighed, axis=1, keepdims=True)).astype(LOW)
        total = total + jnp.dot(
            d_scores,
            only(head_lanes(seq_len, width, head_width, head), keys),
            preferred_element_type=F32,
        )
        dk_sum[...] += lax.dot_general(
            d_scores, only(own, queries), (((0,), (0,)), ((), ())), preferred_element_type=F32
        )
        dv_sum[...] += lax.dot_general(
            prob_low, own_grads, (((0,), (0,)), ((), ())), preferred_element_type=F32
        )
        for part in range(rows // SKEW):
            for at in range(blocks):
                skew_ref[head, :, pl.ds(places[part][at], rows)] += d_scores[
                    part * SKEW : (part + 1) * SKEW, at * rows : (at + 1) * rows
                ].astype(F32)
    d_ref[here, :width] = total.astype(LOW)

    @pl.when(step == pl.num_programs(0) - 1)
    def _():
        d_ref[:, width : 2 * width] = dk_sum[...].astype(LOW)
        d_ref[:, 2 * width :] = dv_sum[...].astype(LOW)
        one_hot = bucket_onehot(dt_ref.shape[0], seq_len)
        row = lax.broadcasted_iota(jnp.int32, (SKEW, span), 0)
        column = lax.broadcasted_iota(jnp.int32, dt_ref.shape, 1)
        result = jnp.zeros(dt_ref.shape, F32)
        for head in range(heads):
            level = pltpu.roll(skew_ref[head], SKEW, 1)
            bit = 1
            while bit < SKEW:
                level = jnp.where((row & bit) != 0, pltpu.roll(level, span - bit, 1), level)
                bit *= 2
            line = jnp.sum(level, axis=0, keepdims=True)
            summed = jnp.sum(jnp.where(one_hot, line, 0.0), axis=1, keepdims=True)
            result = jnp.where(column == head, summed, result)
        dt_ref[...] = result


def attention_backward(prob, mine, other, got, qkv, place, heads, shard, buckets):
    seq_len, width = qkv.shape[0], qkv.shape[1] // 3
    near_count, own_rows, model = mine[0].shape
    count = len(mine)
    rows = count * own_rows
    came_specs, _ = sent_specs(near_count, count, own_rows, model)
    return pl.pallas_call(
        functools.partial(backward_kernel, heads, shard, near_count, count),
        grid=(seq_len // rows,),
        in_specs=[
            pl.BlockSpec(memory_space=pltpu.SMEM),
            *came_specs,
            pl.BlockSpec((heads, rows, seq_len), lambda i: (0, row_block(i, near_count), 0)),
            pl.BlockSpec(got.shape, lambda i: (0, 0, 0)),
            pl.BlockSpec(qkv.shape, lambda i: (0, 0)),
        ],
        out_specs=[
            pl.BlockSpec(qkv.shape, lambda i: (0, 0)),
            pl.BlockSpec((buckets, 128), lambda i: (0, 0)),
            pl.BlockSpec((rows, model), lambda i: (row_block(i, near_count), 0)),
        ],
        out_shape=[
            jax.ShapeDtypeStruct(qkv.shape, LOW),
            jax.ShapeDtypeStruct((buckets, 128), F32),
            jax.ShapeDtypeStruct((seq_len, model), LOW),
        ],
        scratch_shapes=[
            pltpu.VMEM((seq_len, width), F32),
            pltpu.VMEM((seq_len, width), F32),
            pltpu.VMEM((heads, SKEW, 2 * seq_len), F32),
        ],
        compiler_params=pltpu.CompilerParams(vmem_limit_bytes=34 * 2**20),
        cost_estimate=pl.CostEstimate(
            flops=8 * seq_len * seq_len * width * 4,
            bytes_accessed=2 * heads * seq_len * seq_len,
            transcendentals=0,
        ),
        name="attention_backward",
    )(place, *other, *mine, prob, got, qkv)


EXTRA = 8
OWNER_ROWS = 64


def as_column(row, first, count):
    size = row.shape[1]
    here = lax.broadcasted_iota(jnp.int32, (count, size), 1) == first + lax.broadcasted_iota(
        jnp.int32, (count, size), 0
    )
    return jnp.sum(jnp.where(here, row, 0.0), axis=1, keepdims=True)


def blocks_kernel(seqs, members, q_ref, k_ref, v_ref, o_ref, gain_ref, table_ref, sent_ref):
    shard = q_ref.shape[0]
    width = q_ref.shape[1] // members
    gain = as_column(gain_ref[...].astype(LOW).astype(F32), 0, shard)
    parts = [
        (ref[...].astype(LOW).astype(F32) * gain).astype(LOW) for ref in (q_ref, k_ref, v_ref)
    ]
    parts.append(o_ref[...].T.astype(LOW))
    rest = jnp.zeros((EXTRA, sent_ref.shape[2]), LOW)
    table_rows, heads = table_ref.shape
    for seq in range(seqs):
        for member in range(members):
            at = seq * members + member
            for i, part in enumerate(parts):
                sent_ref[at, :shard, i * width : (i + 1) * width] = part[
                    :, member * width : (member + 1) * width
                ]
            sent_ref[at, shard:, :] = rest
            sent_ref[at, shard : shard + table_rows, :heads] = table_ref[...].astype(LOW)


def attention_blocks(weights, w_out, gain, table, seqs, members):
    shard, columns = weights[0].shape
    return pl.pallas_call(
        functools.partial(blocks_kernel, seqs, members),
        out_shape=jax.ShapeDtypeStruct(
            (seqs * members, shard + EXTRA, 4 * columns // members), LOW
        ),
        compiler_params=pltpu.CompilerParams(vmem_limit_bytes=60 * 2**20),
        cost_estimate=pl.CostEstimate(
            flops=0, bytes_accessed=16 * shard * columns, transcendentals=0
        ),
        name="attention_blocks",
    )(*weights, w_out, gain, table)


def owner_kernel(count, members, table_shape, *refs):
    got_ref, extra_ref = refs[:2]
    weight_refs = refs[2 : 2 + count]
    gain_ref = refs[2 + count]
    grad_refs = refs[3 + count : 3 + 2 * count]
    sum_ref = refs[3 + 2 * count]
    step = pl.program_id(0)
    rows = got_ref.shape[1]
    seqs = got_ref.shape[0] // members
    width = got_ref.shape[2] // count
    size = sum_ref.shape[1]
    gain = as_column(gain_ref[...].astype(LOW).astype(F32), step * rows, rows)
    total = jnp.zeros((rows, 1), F32)
    for member in range(members):
        product = sum(got_ref[seq * members + member].astype(F32) for seq in range(seqs))
        for i in range(count):
            part = product[:, i * width : (i + 1) * width]
            here = pl.ds(member * width, width)
            grad_refs[i][:, here] = part * gain
            weight = weight_refs[i][:, here].astype(LOW).astype(F32)
            total = total + jnp.sum(weight * part, axis=1, keepdims=True)

    @pl.when(step == 0)
    def _():
        sum_ref[...] = jnp.zeros_like(sum_ref)

    diagonal = lax.broadcasted_iota(jnp.int32, (rows, size), 1) == step * rows + (
        lax.broadcasted_iota(jnp.int32, (rows, size), 0)
    )
    sum_ref[...] += jnp.sum(jnp.where(diagonal, total, 0.0), axis=0, keepdims=True)
    if table_shape is not None:
        table_rows, heads = table_shape
        each = heads // members
        for member in range(members):
            piece = sum(extra_ref[seq * members + member].astype(F32) for seq in range(seqs))
            refs[-1][:, member * each : (member + 1) * each] = piece[:table_rows, :each]


def owner_grads(got, weights, gain, members, table_shape):
    sources, height, columns = got.shape
    shard, wide = weights[0].shape
    count = len(weights)
    rows = min(OWNER_ROWS, shard)
    step_rows = pl.BlockSpec((rows, wide), lambda i: (i, 0))
    row = pl.BlockSpec((1, shard), lambda i: (0, 0))
    last = height // EXTRA - 1
    out_specs = [step_rows] * count + [row]
    out_shape = [jax.ShapeDtypeStruct((shard, wide), F32)] * count
    out_shape.append(jax.ShapeDtypeStruct((1, shard), F32))
    if table_shape is not None:
        out_specs.append(pl.BlockSpec(table_shape, lambda i: (0, 0)))
        out_shape.append(jax.ShapeDtypeStruct(table_shape, F32))
    outs = pl.pallas_call(
        functools.partial(owner_kernel, count, members, table_shape),
        grid=(shard // rows,),
        in_specs=[
            pl.BlockSpec((sources, rows, columns), lambda i: (0, i, 0)),
            pl.BlockSpec((sources, EXTRA, columns), lambda i: (0, last, 0)),
        ]
        + [step_rows] * count
        + [row],
        out_specs=out_specs,
        out_shape=out_shape,
        compiler_params=pltpu.CompilerParams(vmem_limit_bytes=32 * 2**20),
        cost_estimate=pl.CostEstimate(
            flops=0, bytes_accessed=10 * count * shard * wide, transcendentals=0
        ),
        name="owner_grads",
    )(got, got, *weights, gain)
    return outs[:count], outs[count], outs[-1] if table_shape is not None else None


def rows_dot(left, right):
    return jnp.dot(left, right, preferred_element_type=F32)


def contract_cols(left, right):
    return lax.dot_general(left, right, (((1,), (1,)), ((), ())), preferred_element_type=F32)


def contract_rows(left, right):
    return lax.dot_general(left, right, (((0,), (0,)), ((), ())), preferred_element_type=F32)

def row_block(step, near_count):
    return lax.rem(step + near_count, CORES * near_count)


def send_rows(step, near_count, mp_at, held_ref, other_refs, mine_refs):
    count = len(other_refs)
    own_rows = held_ref.shape[0] // count

    def write(refs):
        for away, ref in enumerate(refs):
            first = pl.multiple_of(lax.bitwise_xor(mp_at, away) * own_rows, own_rows)
            ref[0] = held_ref[pl.ds(first, own_rows), :]

    @pl.when(step < near_count)
    def _():
        write(other_refs)

    @pl.when(step >= near_count)
    def _():
        write(mine_refs)


def take_rows(step, near_count, mp_at, other_refs, mine_refs, rows_ref):
    own_rows = other_refs[0].shape[1]

    def read(refs):
        for away, ref in enumerate(refs):
            first = pl.multiple_of(lax.bitwise_xor(mp_at, away) * own_rows, own_rows)
            rows_ref[pl.ds(first, own_rows), :] = ref[0]

    @pl.when(step < near_count)
    def _():
        read(other_refs)

    @pl.when(step >= near_count)
    def _():
        read(mine_refs)


def sent_specs(near_count, count, own_rows, model):
    other = pl.BlockSpec((1, own_rows, model), lambda i: (jnp.minimum(i, near_count - 1), 0, 0))
    mine = pl.BlockSpec((1, own_rows, model), lambda i: (jnp.maximum(i - near_count, 0), 0, 0))
    shape = jax.ShapeDtypeStruct((near_count, own_rows, model), LOW)
    return [other] * count + [mine] * count, [shape] * (2 * count)


def partial_kernel(near_count, count, product, place_ref, left_ref, weight_ref, *refs):
    held_ref = refs[-1]
    product(left_ref, weight_ref, held_ref)
    send_rows(
        pl.program_id(0), near_count, place_ref[3], held_ref, refs[:count], refs[count : 2 * count]
    )


def partial_rows(left, weight, model, place, near_count, count, product, name):
    seq_len, depth = left.shape
    rows = seq_len // (CORES * near_count)
    out_specs, out_shape = sent_specs(near_count, count, rows // count, model)
    outs = pl.pallas_call(
        functools.partial(partial_kernel, near_count, count, product),
        grid=(CORES * near_count,),
        in_specs=[
            pl.BlockSpec(memory_space=pltpu.SMEM),
            pl.BlockSpec((rows, depth), lambda i: (row_block(i, near_count), 0)),
            pl.BlockSpec(weight.shape, lambda i: (0, 0, 0)),
        ],
        out_specs=out_specs,
        out_shape=out_shape,
        scratch_shapes=[pltpu.VMEM((rows, model), LOW)],
        compiler_params=pltpu.CompilerParams(vmem_limit_bytes=40 * 2**20),
        cost_estimate=pl.CostEstimate(
            flops=2 * seq_len * depth * model, bytes_accessed=2 * seq_len * model, transcendentals=0
        ),
        name=name,
    )(place, left, weight)
    return outs[count:], outs[:count]


def column_product(shard, first, last, left_ref, weight_ref, held_ref):
    weight = weight_ref[:, :shard, first:last]
    weight = weight.reshape(weight.shape[0] * shard, last - first)
    held_ref[...] = contract_cols(left_ref[...], weight).astype(LOW)


def row_product(height, left_ref, weight_ref, held_ref):
    left = left_ref[...]
    width = weight_ref.shape[2]
    for at in range(weight_ref.shape[0]):
        held_ref[:, at * width : (at + 1) * width] = rows_dot(
            left, weight_ref[at, :height, :]
        ).astype(LOW)


def ffn_blocks_kernel(seqs, members, gate_ref, up_ref, down_ref, gain_ref, first_ref, second_ref):
    shard = gate_ref.shape[0]
    width = gate_ref.shape[1] // members
    gain = as_column(gain_ref[...].astype(LOW).astype(F32), 0, shard)
    for member in range(members):
        here = slice(member * width, (member + 1) * width)
        parts = [
            (ref[:, here].astype(LOW).astype(F32) * gain).astype(LOW) for ref in (gate_ref, up_ref)
        ]
        both = jnp.concatenate(parts, 1)
        down = down_ref[here, :].astype(LOW)
        for seq in range(seqs):
            at = seq * members + member
            first_ref[at, :width, :] = down
            first_ref[at, width:, :] = both[:, :shard]
            second_ref[at] = both[:, shard:]


def ffn_blocks(w_gate, w_up, w_down, gain, seqs, members):
    shard, columns = w_gate.shape
    width = columns // members
    return pl.pallas_call(
        functools.partial(ffn_blocks_kernel, seqs, members),
        out_shape=[
            jax.ShapeDtypeStruct((seqs * members, width + shard, shard), LOW),
            jax.ShapeDtypeStruct((seqs * members, shard, 2 * width - shard), LOW),
        ],
        compiler_params=pltpu.CompilerParams(vmem_limit_bytes=40 * 2**20),
        cost_estimate=pl.CostEstimate(
            flops=0, bytes_accessed=18 * shard * columns, transcendentals=0
        ),
        name="ffn_blocks",
    )(w_gate, w_up, w_down, gain)


def ffn_kernel(near_count, count, place_ref, *refs):
    came, refs = refs[: 2 * count], refs[2 * count :]
    grad_ref, first_ref, second_ref = refs[:3]
    other_refs, mine_refs = refs[3 : 3 + count], refs[3 + count : 3 + 2 * count]
    rows_ref, act_ref, d_ref, down_ref, held_ref, sum_ref = refs[3 + 2 * count :]
    step = pl.program_id(0)
    take_rows(step, near_count, place_ref[3], came[:count], came[count:], rows_ref)
    sources, height, shard = first_ref.shape
    width = height - shard
    rows = rows_ref[...]
    block = row_block(step, near_count)
    first = block_place(block, place_ref[1], near_count) * rows.shape[0]
    valid = first + lax.broadcasted_iota(jnp.int32, (rows.shape[0], 1), 0) < place_ref[0]
    grads = only(valid, grad_ref[...])
    early = first_ref[:, width:, :].reshape(sources * shard, shard)
    late = second_ref[...].reshape(sources * shard, 2 * width - shard)
    both = jnp.concatenate([rows_dot(rows, early), rows_dot(rows, late)], 1)
    gate, up = both[:, :width], both[:, width:]
    scale, cubic = 0.7978845608028654, 0.044715
    square = gate * gate
    bent = jnp.tanh(scale * (gate + cubic * square * gate))
    half = 0.5 * (1.0 + bent)
    value = gate * half
    slope = half + 0.5 * gate * (1.0 - bent * bent) * (scale * (1.0 + 3.0 * cubic * square))
    act = (value * up).astype(LOW)
    act_ref[...] = act
    d_hidden = jnp.zeros((rows.shape[0], width), F32)
    for at in range(sources):
        d_hidden = d_hidden + contract_cols(
            grads[:, at * shard : (at + 1) * shard], first_ref[at, :width, :]
        )
    d_both = jnp.concatenate(
        [(d_hidden * up * slope).astype(LOW), (d_hidden * value).astype(LOW)], 1
    )
    d_ref[...] = d_both
    held_ref[...] = (
        contract_cols(d_both[:, :shard], early) + contract_cols(d_both[:, shard:], late)
    ).astype(LOW)
    send_rows(step, near_count, place_ref[3], held_ref, other_refs, mine_refs)
    product = contract_rows(act, grads)

    @pl.when(step == 0)
    def _():
        sum_ref[...] = product

    @pl.when(step > 0)
    def _():
        sum_ref[...] += product

    @pl.when(step == pl.num_programs(0) - 1)
    def _():
        for at in range(sources):
            down_ref[at] = sum_ref[:, at * shard : (at + 1) * shard].astype(LOW)


def feed_forward(mine, other, grads, first, second, place):
    seq_len, model = grads.shape
    near_count, count = mine[0].shape[0], len(mine)
    sources, height, shard = first.shape
    width = height - shard
    rows = seq_len // (CORES * near_count)
    out_specs, out_shape = sent_specs(near_count, count, rows // count, model)

    def blocks(columns):
        return pl.BlockSpec((rows, columns), lambda i: (row_block(i, near_count), 0))

    outs = pl.pallas_call(
        functools.partial(ffn_kernel, near_count, count),
        grid=(CORES * near_count,),
        in_specs=[
            pl.BlockSpec(memory_space=pltpu.SMEM),
            *out_specs,
            blocks(model),
            pl.BlockSpec(first.shape, lambda i: (0, 0, 0)),
            pl.BlockSpec(second.shape, lambda i: (0, 0, 0)),
        ],
        out_specs=out_specs
        + [
            blocks(model),
            blocks(width),
            blocks(2 * width),
            pl.BlockSpec((sources, width, shard), lambda i: (0, 0, 0)),
        ],
        out_shape=out_shape
        + [
            jax.ShapeDtypeStruct((seq_len, model), LOW),
            jax.ShapeDtypeStruct((seq_len, width), LOW),
            jax.ShapeDtypeStruct((seq_len, 2 * width), LOW),
            jax.ShapeDtypeStruct((sources, width, shard), LOW),
        ],
        scratch_shapes=[pltpu.VMEM((rows, model), LOW), pltpu.VMEM((width, model), F32)],
        compiler_params=pltpu.CompilerParams(vmem_limit_bytes=56 * 2**20),
        cost_estimate=pl.CostEstimate(
            flops=12 * seq_len * model * width, bytes_accessed=12 * seq_len * model, transcendentals=0
        ),
        name="feed_forward",
    )(place, *other, *mine, grads, first, second)
    return outs[count : 2 * count], outs[:count], *outs[2 * count :]


COLUMN = ("seq", "near", "core")


def exchange(blocks, axes):
    return lax.all_to_all(blocks, axes, split_axis=0, concat_axis=0, tiled=True)


def swap(block, axis):
    return lax.ppermute(block, axis, [(0, 1), (1, 0)])


def after(value, *done):
    return lax.optimization_barrier((value,) + done)[0]


def rms(values):
    return lax.rsqrt(jnp.mean(values * values, axis=-1, keepdims=True) + EPSILON)


def norm_grad(inner, normed, inverse):
    return inverse * (inner - normed * jnp.mean(inner * normed, axis=-1, keepdims=True))


def local(
    inputs,
    cotangent,
    lengths,
    attn_scale,
    w_query,
    w_key,
    w_value,
    w_out,
    rel_table,
    ffn_scale,
    w_gate,
    w_up,
    w_down,
):
    seqs = lax.axis_size("seq")
    near_count = lax.axis_size("near")
    mp_count = lax.axis_size("mp")
    members = near_count * CORES
    sources = seqs * members
    tok_rows, model = inputs.shape
    seq_len = tok_rows * members
    own_rows = tok_rows // mp_count
    half_rows = seq_len // CORES
    shard = attn_scale.shape[0]
    table_rows, heads_mp = rel_table.shape
    buckets = table_rows * sources
    heads = heads_mp // members
    width = w_query.shape[1] // members
    hidden_width = w_gate.shape[1] // members

    near_at = lax.axis_index("near")
    core_at = lax.axis_index("core")
    mp_at = lax.axis_index("mp")
    member_at = near_at * CORES + core_at
    length = lax.dynamic_slice_in_dim(lengths, lax.axis_index("seq"), 1, 0)
    place = jnp.stack(
        [length[0]] + [at.astype(jnp.int32) for at in (core_at, member_at, mp_at, near_at)]
    )

    def over_mp(own, axis):
        shape = own.shape[:axis] + (mp_count,) + own.shape[axis:]
        blocks = lax.dynamic_update_index_in_dim(jnp.zeros(shape, own.dtype), own, mp_at, axis)
        moved = [(away, shifted(own, away)) for away in reversed(range(1, mp_count))]
        for away, block in moved:
            blocks = lax.dynamic_update_index_in_dim(blocks, block, mp_at ^ away, axis)
        return blocks

    def shifted(block, away):
        return lax.ppermute(block, "mp", [(i, i ^ away) for i in range(mp_count)])

    def in_near_order(own, moved):
        return jnp.stack(
            [jnp.where(near_at == 0, own, moved), jnp.where(near_at == 0, moved, own)], 0
        )

    def near_rows(blocks):
        own = [lax.dynamic_slice_in_dim(block, mp_at * own_rows, own_rows, 0) for block in blocks]
        near = swap(jnp.stack(own), "near")
        came = [(0, near)] + [(away, shifted(near, away)) for away in range(1, mp_count)]
        halves = []
        for half in (came, [(away, swap(block, "core")) for away, block in came]):
            rows = jnp.zeros((len(blocks), mp_count, own_rows, model), near.dtype)
            for away, block in half:
                rows = lax.dynamic_update_index_in_dim(rows, block, mp_at ^ away, 1)
            halves.append([rows[i].reshape(tok_rows, model) for i in range(len(blocks))])
        return *halves, came[1][1]

    def in_order(own, moved, core, core_moved):
        rows = jnp.zeros((CORES, near_count, tok_rows, model), own.dtype)
        for at, block in enumerate((own, moved, core, core_moved)):
            rows = lax.dynamic_update_slice(
                rows, block[None, None], (at // 2, near_at ^ (at % 2), 0, 0)
            )
        return rows.reshape(seq_len, model)

    def gather_rows(near):
        mine = [near] + [shifted(near, away) for away in range(1, mp_count)]
        return mine, [swap(block, "core") for block in mine]

    def sum_cores(mine, other):
        return [
            kept.astype(F32) + swap(sent, "core").astype(F32) for kept, sent in zip(mine, other)
        ]

    def send_mp(sums):
        return [shifted(sums[away].astype(LOW), away) for away in reversed(range(1, mp_count))]

    def sum_mp(sums, *meanwhile):
        moved = send_mp(sums)
        if meanwhile:
            moved = [after(piece, *meanwhile) for piece in moved]
        return sum((piece.astype(F32) for piece in moved), sums[0])

    def split_near(pair):
        sent = jnp.where(near_at == 0, pair[1], pair[0]).astype(LOW)
        return sent, jnp.where(near_at == 0, pair[0], pair[1])

    def sum_near_both(pair):
        low = pair.astype(LOW)
        moved = swap(low, "near")
        return low.astype(F32) + moved.astype(F32), moved

    def near_pair(own, moved):
        pair = [
            lax.dynamic_slice_in_dim(block, mp_at * own_rows, own_rows, 0)
            for block in (own, moved)
        ]
        return in_near_order(*pair)

    def here(pair):
        return lax.dynamic_index_in_dim(pair, near_at, 0, keepdims=False)

    attn_sent = attention_blocks(
        (w_query, w_key, w_value), w_out, attn_scale.reshape(1, shard), rel_table, seqs, members
    )
    attn_got = exchange(attn_sent, COLUMN)
    def partial(left, weight, product, name):
        return partial_rows(left, weight, model, place, near_count, mp_count, product, name)

    table = attn_got[:, shard : shard + table_rows, :heads_mp].reshape(buckets, heads_mp)

    def normed(rows):
        values = rows.astype(F32)
        return (values * rms(values)).astype(LOW)

    (moved_inputs, moved_cotangent), core_moved, first_came = near_rows([inputs, cotangent])
    input_parts = [inputs, moved_inputs, swap(inputs, "core"), core_moved[0]]
    core_cotangent = swap(after(cotangent, moved_inputs), "core")
    grad_parts = [cotangent, moved_cotangent, core_cotangent, core_moved[1]]
    ffn_first, ffn_second = ffn_blocks(
        w_gate, w_up, w_down, after(ffn_scale.reshape(1, shard), first_came), seqs, members
    )
    parts = [normed(part) for part in input_parts]
    parts = lax.optimization_barrier((*parts, ffn_first, ffn_second))[:4]
    first_got = exchange(after(ffn_first, attn_got), COLUMN)

    qkv, attended, prob, out_mine, out_other = attention_forward(
        parts, attn_got, table, place, heads, shard, mp_count
    )
    normed_rows, grad_two = in_order(*parts), in_order(*grad_parts)
    mixed, mixed_moved = sum_near_both(
        after(sum_mp(sum_cores(out_mine, out_other)), first_got, grad_two, normed_rows)
    )
    second_got = exchange(after(ffn_second, mixed_moved), COLUMN)

    pair_inputs = near_pair(inputs, moved_inputs).astype(F32)
    after_attn = pair_inputs + mixed
    inv_two = rms(after_attn)
    normed_two = after_attn * inv_two
    mine_two, other_two = gather_rows(normed_two.astype(LOW))

    d_mine, d_other, hidden_two, acts, d_both, d_down_w = feed_forward(
        mine_two, other_two, grad_two, first_got, second_got, place
    )
    inner_cores = sum_cores(d_mine, d_other)
    down_product = functools.partial(row_product, hidden_width)
    ffn_partial = partial(after(acts, *inner_cores), first_got, down_product, "ffn_out")

    def to_owners(grad):
        return exchange(grad, COLUMN)

    def by_rows(got):
        parts = got.reshape((seqs, members) + got.shape[1:]).astype(F32)
        return jnp.sum(parts, axis=0).reshape(-1, shard)

    d_gate_up_w = contract_rows(hidden_two, after(d_both, *inner_cores)).astype(LOW)
    inner_two, inner_moved = sum_near_both(
        sum_mp(inner_cores, d_gate_up_w, *ffn_partial[0], *ffn_partial[1])
    )

    pair_first = (
        lax.broadcasted_iota(jnp.int32, (near_count, own_rows, 1), 0) * (CORES * tok_rows)
        + lax.broadcasted_iota(jnp.int32, (near_count, own_rows, 1), 1)
        + (core_at * tok_rows + mp_at * own_rows)
    )
    pair_valid = pair_first < length
    pair_grad = near_pair(cotangent, moved_cotangent).astype(F32)
    grad_one = jnp.where(pair_valid, pair_grad, 0.0) + norm_grad(inner_two, normed_two, inv_two)
    grad_one_low = grad_one.astype(LOW)
    mine_one, other_one = gather_rows(grad_one_low)
    d_gate_up = to_owners(
        after(d_gate_up_w, inner_moved, grad_one_low).reshape(sources, shard, -1)
    )
    ffn_cores = sum_cores(*ffn_partial)
    d_qkv, d_table, rows_one = attention_backward(
        prob, mine_one, other_one, attn_got, qkv, place, heads, shard, buckets
    )
    qkv_product = functools.partial(column_product, shard, 0, 3 * width)
    ffn_moved = send_mp([after(rows, *mine_one[1:]) for rows in ffn_cores])
    inner_cores = sum_cores(
        *partial(after(d_qkv, *ffn_moved), attn_got, qkv_product, "attention_in")
    )
    inner_pair = sum_mp(inner_cores)
    table_sent = d_table[:, :heads].astype(LOW).reshape(sources, table_rows, heads)
    table_sent = jnp.pad(
        table_sent, ((0, 0), (0, EXTRA - table_rows), (0, 3 * width - heads))
    )
    d_qkv_w = contract_rows(normed_rows, d_qkv).astype(LOW).reshape(sources, shard, -1)
    d_qkv_sent = jnp.concatenate([d_qkv_w, table_sent], 1)
    d_qkv_got = to_owners(after(d_qkv_sent, d_gate_up))
    d_out = contract_rows(after(attended, inner_cores[0]), rows_one)
    d_out = jnp.moveaxis(d_out.astype(LOW).reshape(width, sources, shard), 1, 0)

    (d_w_gate, d_w_up), ffn_gain, _ = owner_grads(
        after(d_gate_up, inner_cores[0]), (w_gate, w_up), ffn_scale.reshape(1, shard), members, None
    )
    ffn_sent, ffn_kept = split_near(
        sum((piece.astype(F32) for piece in ffn_moved), ffn_cores[0])
    )
    inner_sent, inner_kept = split_near(inner_pair)
    came = swap(
        after(jnp.stack([ffn_sent, inner_sent]), d_qkv_got, ffn_gain), "near"
    )
    own_inputs = here(pair_inputs)
    inv_one = rms(own_inputs)
    grad_input = here(grad_one) + norm_grad(inner_kept + came[1].astype(F32), own_inputs * inv_one, inv_one)
    own_out = jnp.where(here(pair_valid), here(after_attn) + ffn_kept + came[0].astype(F32), 0.0)
    owned = jnp.stack([own_out.astype(LOW), grad_input.astype(LOW)])
    rows_out = [jnp.zeros((mp_count, own_rows, model), LOW)] * 2
    blocks_out = [owned] + [shifted(owned, away) for away in range(1, mp_count)]
    d_rows = to_owners(after(jnp.concatenate([d_down_w, d_out], 1), d_qkv_got))
    for away, block in enumerate(blocks_out):
        rows_out = [
            lax.dynamic_update_index_in_dim(rows, block[i], mp_at ^ away, 0)
            for i, rows in enumerate(rows_out)
        ]
    layer_out, d_inputs = (rows.reshape(tok_rows, model) for rows in rows_out)

    (d_w_query, d_w_key, d_w_value), attn_gain, d_rel_table = owner_grads(
        after(d_qkv_got, blocks_out[1]),
        (w_query, w_key, w_value),
        attn_scale.reshape(1, shard),
        members,
        (table_rows, heads_mp),
    )
    gains = jnp.concatenate([attn_gain, ffn_gain], 0)
    gains = sum((shifted(gains, away) for away in range(1, mp_count)), gains)
    return (
        layer_out,
        d_inputs,
        gains[0],
        d_w_query,
        d_w_key,
        d_w_value,
        by_rows(d_rows[:, hidden_width:]),
        d_rel_table,
        gains[1],
        d_w_gate,
        d_w_up,
        by_rows(d_rows[:, :hidden_width]),
    )


def solution(mesh):
    fsdp, mp = mesh.shape["fsdp"], mesh.shape["mp"]

    def run(*args):
        seqs = args[2].shape[0]
        members = fsdp // seqs
        inner = Mesh(
            mesh.devices.reshape(seqs, members // CORES, CORES, mp), ("seq", "near", "core", "mp")
        )
        rows, columns, first = P(COLUMN, None), P("mp", COLUMN), P(COLUMN)
        both = P(COLUMN, "mp")
        in_specs = (
            rows, rows, P(), first, both, both, both, columns, both, first, both, both, columns,
        )
        out_specs = (
            rows, rows, first, both, both, both, columns, both, first, both, both, columns,
        )
        return jax.shard_map(
            local, mesh=inner, in_specs=in_specs, out_specs=out_specs, check_vma=False
        )(*args)

    return run
```

profile of v0, /device:TPU:0, one launch (start us, length us, event | category | flops | bytes accessed | tf_op | source)
XLA Modules:
  0.0 431.8 jit_solution(14954368402036917362)
XLA Ops:
  14.1 6.1 %collective-permute-done = bf16[2,64,2048]{2,1,0:T(8,128)(2,1)} collective-permute-done((bf16[2,64,2048]{2,1,0:T(8,128)(2,1)S(1)}, bf16[2,64,2048]{2,1,0:T(8,128)(2,1)}, u32[]{:S(2)}, u32[]{:S(2)}) %collective-permute-start) | collective-permute-done | bytes 524320 | tf_op jit(solution)/shard_map/ppermute | solution.py:658
  35.3 18.9 %collective-permute-done.2 = bf16[2,64,2048]{2,1,0:T(8,128)(2,1)S(1)} collective-permute-done((bf16[2,64,2048]{2,1,0:T(8,128)(2,1)}, bf16[2,64,2048]{2,1,0:T(8,128)(2,1)S(1)}, u32[]{:S(2)}, u32[]{:S(2)}) %collective-permute-start.2) | collective-permute-done | bytes 524320 | tf_op jit(solution)/shard_map/ppermute | solution.py:722
  71.8 7.4 %all-to-all-start.1 = ((bf16[8,576,256]{2,1,0:T(8,128)(2,1)}), bf16[8,576,256]{2,1,0:T(8,128)(2,1)}, u32[]{:S(2)}, u32[]{:S(2)}) async-start(bf16[8,576,256]{2,1,0:T(8,128)(2,1)} %copy-done.6), calls=%async_computation.1 | async-start | bytes 4718592 | tf_op jit(solution)/shard_map/all_to_all | solution.py:654
  83.0 11.8 %attention_forward.1 = (bf16[1024,384]{1,0:T(8,128)(2,1)S(1)}, bf16[1024,128]{1,0:T(8,128)(2,1)S(1)}, bf16[2,1024,1024]{2,1,0:T(8,128)(2,1)S(1)}, bf16[2,64,2048...) custom-call(s32[5]{0:T(128)S(1)} %stack.62.place_ref, ...), custom_call_target="tpu_custom_call" | custom-call | tf_op jit(solution)/shard_map/attention_forward/pallas_call | solution.py:146
  105.7 8.5 %collective-permute-done.11 = bf16[2,64,2048]{2,1,0:T(8,128)(2,1)S(1)} collective-permute-done((bf16[2,64,2048]{2,1,0:T(8,128)(2,1)S(1)}, bf16[2,64,2048]{2,1,0:T(8,128)(2,1)S(1)}, u32[]{:S(2)}, u32[]{:S(2)}) %collective-permute-start.11) | collective-permute-done | bytes 524320 | tf_op jit(solution)/shard_map/ppermute | solution.py:722
  114.2 10.8 %collective-permute-done.13 = bf16[2,64,2048]{2,1,0:T(8,128)(2,1)S(1)} collective-permute-done((bf16[2,64,2048]{2,1,0:T(8,128)(2,1)S(1)}, bf16[2,64,2048]{2,1,0:T(8,128)(2,1)S(1)}, u32[]{:S(2)}, u32[]{:S(2)}) %collective-permute-start.13) | collective-permute-done | bytes 524320 | tf_op jit(solution)/shard_map/ppermute | solution.py:722
  125.5 8.5 %all-to-all-done.1.refs_9_.weight_ref = bf16[8,576,256]{2,1,0:T(8,128)(2,1)} async-done(((bf16[8,576,256]{2,1,0:T(8,128)(2,1)}), bf16[8,576,256]{2,1,0:T(8,128)(2,1)}, u32[]{:S(2)}, u32[]{:S(2)}) %all-to-all-start.1) | async-done | bytes 2359328 | tf_op jit(solution)/shard_map/all_to_all | solution.py:654
  134.0 13.5 %collective-permute-done.17 = bf16[2,64,2048]{2,1,0:T(8,128)(2,1)S(1)} collective-permute-done((bf16[2,64,2048]{2,1,0:T(8,128)(2,1)S(1)}, bf16[2,64,2048]{2,1,0:T(8,128)(2,1)S(1)}, u32[]{:S(2)}, u32[]{:S(2)}) %collective-permute-start.17) | collective-permute-done | bytes 524320 | tf_op jit(solution)/shard_map/ppermute | solution.py:658
  157.4 11.2 %collective-permute-done.19.refs_5_ = bf16[2,64,2048]{2,1,0:T(8,128)(2,1)S(1)} collective-permute-done((bf16[2,64,2048]{2,1,0:T(8,128)(2,1)S(1)}, bf16[2,64,2048]{2,1,0:T(8,128)(2,1)S(1)}, u32[]{:S(2)}, u32[]{:S(2)}) %collective-permute-start.19) | collective-permute-done | bytes 524320 | tf_op jit(solution)/shard_map/ppermute | solution.py:722
  168.6 10.1 %collective-permute-done.21.refs_6_ = bf16[2,64,2048]{2,1,0:T(8,128)(2,1)S(1)} collective-permute-done((bf16[2,64,2048]{2,1,0:T(8,128)(2,1)S(1)}, bf16[2,64,2048]{2,1,0:T(8,128)(2,1)S(1)}, u32[]{:S(2)}, u32[]{:S(2)}) %collective-permute-start.21) | collective-permute-done | bytes 524320 | tf_op jit(solution)/shard_map/ppermute | solution.py:722
  182.4 7.4 %all-to-all-done.2.refs_10_ = bf16[8,256,384]{2,1,0:T(8,128)(2,1)} async-done(((bf16[8,256,384]{2,1,0:T(8,128)(2,1)}), bf16[8,256,384]{2,1,0:T(8,128)(2,1)}, u32[]{:S(2)}, u32[]{:S(2)}) %all-to-all-start.2) | async-done | bytes 1572896 | tf_op jit(solution)/shard_map/all_to_all | solution.py:654
  189.8 19.9 %feed_forward.1 = (bf16[2,64,2048]{2,1,0:T(8,128)(2,1)}, bf16[2,64,2048]{2,1,0:T(8,128)(2,1)}, bf16[2,64,2048]{2,1,0:T(8,128)(2,1)}, bf16[2,64,2048]{2,1,0:T(8,1...) custom-call(s32[5]{0:T(128)} %copy-done.23, ...), custom_call_target="tpu_custom_call" | custom-call | flops 8053063680 | bytes 25165824 | tf_op jit(solution)/shard_map/feed_forward/pallas_call | solution.py:616
  231.2 10.4 %collective-permute-done.32 = bf16[2,64,2048]{2,1,0:T(8,128)(2,1)S(1)} collective-permute-done((bf16[2,64,2048]{2,1,0:T(8,128)(2,1)S(1)}, bf16[2,64,2048]{2,1,0:T(8,128)(2,1)S(1)}, u32[]{:S(2)}, u32[]{:S(2)}) %collective-permute-start.32) | collective-permute-done | bytes 524320 | tf_op jit(solution)/shard_map/ppermute | solution.py:722
  244.0 11.9 %collective-permute-done.34 = bf16[2,64,2048]{2,1,0:T(8,128)(2,1)S(1)} collective-permute-done((bf16[2,64,2048]{2,1,0:T(8,128)(2,1)S(1)}, bf16[2,64,2048]{2,1,0:T(8,128)(2,1)S(1)}, u32[]{:S(2)}, u32[]{:S(2)}) %collective-permute-start.34) | collective-permute-done | bytes 524320 | tf_op jit(solution)/shard_map/ppermute | solution.py:658
  269.1 8.6 %collective-permute-done.35.refs_5_ = bf16[2,64,2048]{2,1,0:T(8,128)(2,1)S(1)} collective-permute-done((bf16[2,64,2048]{2,1,0:T(8,128)(2,1)}, bf16[2,64,2048]{2,1,0:T(8,128)(2,1)S(1)}, u32[]{:S(2)}, u32[]{:S(2)}) %collective-permute-start.35) | collective-permute-done | bytes 524320 | tf_op jit(solution)/shard_map/ppermute | solution.py:722
  279.1 11.4 %collective-permute-done.36.refs_6_ = bf16[2,64,2048]{2,1,0:T(8,128)(2,1)S(1)} collective-permute-done((bf16[2,64,2048]{2,1,0:T(8,128)(2,1)}, bf16[2,64,2048]{2,1,0:T(8,128)(2,1)S(1)}, u32[]{:S(2)}, u32[]{:S(2)}) %collective-permute-start.36) | collective-permute-done | bytes 524320 | tf_op jit(solution)/shard_map/ppermute | solution.py:722
  296.7 15.0 %attention_backward.1 = (bf16[1024,384]{1,0:T(8,128)(2,1)S(1)}, f32[32,128]{1,0:T(8,128)S(1)}, bf16[1024,2048]{1,0:T(8,128)(2,1)S(1)}) custom-call(s32[5]{0:T(128)S(1)} %copy-done.24, bf16[2,64,2048]{2,1,0:T(8,128)(2,1)S(1)} %collective-permute-done.43.refs_0_, bf16[2,64,2048]{2,1,0:T(8,128)(2,1)S(1)} %collective-permute-done.44.refs_1_, ...), custom_call_target="tpu_custom_call" | custom-call | flops 4294967296 | bytes 4194304 | tf_op jit(solution)/shard_map/attention_backward/pallas_call | solution.py:256
  317.5 6.0 %attention_in.1 = (bf16[2,64,2048]{2,1,0:T(8,128)(2,1)}, bf16[2,64,2048]{2,1,0:T(8,128)(2,1)}, bf16[2,64,2048]{2,1,0:T(8,128)(2,1)}, bf16[2,64,2048]{2,1,0:T(8,1...) custom-call(s32[5]{0:T(128)S(1)} %copy-done.24, ...), custom_call_target="tpu_custom_call" | custom-call | flops 1610612736 | bytes 4194304 | tf_op jit(solution)/shard_map/attention_in/pallas_call | solution.py:480
  332.2 5.4 %all-to-all-start.4 = ((bf16[8,264,384]{2,1,0:T(8,128)(2,1)}), bf16[8,264,384]{2,1,0:T(8,128)(2,1)}, u32[]{:S(2)}, u32[]{:S(2)}) async-start(bf16[8,264,384]{2,1,0:T(8,128)(2,1)} %fusion.6), calls=%async_computation.4 | async-start | bytes 3244032 | tf_op jit(solution)/shard_map/all_to_all | solution.py:654
  346.7 10.2 %collective-permute-done.51 = bf16[2,64,2048]{2,1,0:T(8,128)(2,1)S(1)} collective-permute-done((bf16[2,64,2048]{2,1,0:T(8,128)(2,1)S(1)}, bf16[2,64,2048]{2,1,0:T(8,128)(2,1)S(1)}, u32[]{:S(2)}, u32[]{:S(2)}) %collective-permute-start.51) | collective-permute-done | bytes 524320 | tf_op jit(solution)/shard_map/ppermute | solution.py:722
  365.2 11.3 %all-to-all-done.4.refs_0_.refs_1_ = bf16[8,264,384]{2,1,0:T(8,128)(2,1)} async-done(((bf16[8,264,384]{2,1,0:T(8,128)(2,1)}), bf16[8,264,384]{2,1,0:T(8,128)(2,1)}, u32[]{:S(2)}, u32[]{:S(2)}) %all-to-all-start.4) | async-done | bytes 1622048 | tf_op jit(solution)/shard_map/all_to_all | solution.py:654
  385.9 6.5 %collective-permute-done.54 = bf16[2,64,2048]{2,1,0:T(8,128)(2,1)} collective-permute-done((bf16[2,64,2048]{2,1,0:T(8,128)(2,1)}, bf16[2,64,2048]{2,1,0:T(8,128)(2,1)}, u32[]{:S(2)}, u32[]{:S(2)}) %collective-permute-start.54) | collective-permute-done | bytes 524320 | tf_op jit(solution)/shard_map/ppermute | solution.py:658
  400.3 11.4 %collective-permute-done.55 = bf16[2,64,2048]{2,1,0:T(8,128)(2,1)S(1)} collective-permute-done((bf16[2,64,2048]{2,1,0:T(8,128)(2,1)S(1)}, bf16[2,64,2048]{2,1,0:T(8,128)(2,1)S(1)}, u32[]{:S(2)}, u32[]{:S(2)}) %collective-permute-start.55) | collective-permute-done | bytes 524320 | tf_op jit(solution)/shard_map/ppermute | solution.py:722
  422.8 6.5 %all-to-all-done.5 = bf16[8,448,256]{2,1,0:T(8,128)(2,1)S(1)} async-done(((bf16[8,448,256]{2,1,0:T(8,128)(2,1)}), bf16[8,448,256]{2,1,0:T(8,128)(2,1)S(1)}, u32[]{:S(2)}, u32[]{:S(2)}) %all-to-all-start.5) | async-done | bytes 1835040 | tf_op jit(solution)/shard_map/all_to_all | solution.py:654
  (365 shorter events, 180.9 us)
Async XLA Ops:
  0.6 55.0 %collective-permute-start.4 = (bf16[256,2048]{1,0:T(8,128)(2,1)}, bf16[256,2048]{1,0:T(8,128)(2,1)}, u32[]{:S(2)}, u32[]{:S(2)}) collective-permute-start(bf16[256,2048]{1,0:T(8,128)(2,1)} %param.13), channel_id=1, source_target_pairs={{0,4},{4,0},{1,5},{5,1},{2,6},{6,2},{3,7},{7,3},{8,12},{12,8},{9,1... | collective-permute-start | bytes 3145736 | tf_op jit(solution)/shard_map/ppermute | solution.py:658
  9.1 62.7 %all-to-all-start = ((bf16[8,264,512]{2,1,0:T(8,128)(2,1)}), bf16[8,264,512]{2,1,0:T(8,128)(2,1)}, u32[]{:S(2)}, u32[]{:S(2)}) async-start(bf16[8,264,512]{2,1,0:T(8,128)(2,1)} %attention_blocks.1), calls=%async_computation | async-start | bytes 4325376 | tf_op jit(solution)/shard_map/all_to_all | solution.py:654
  28.4 35.6 %collective-permute-start.5 = (bf16[2,64,2048]{2,1,0:T(8,128)(2,1)}, bf16[2,64,2048]{2,1,0:T(8,128)(2,1)}, u32[]{:S(2)}, u32[]{:S(2)}) collective-permute-start(bf16[2,64,2048]{2,1,0:T(8,128)(2,1)} %collective-permute-done), channel_id=1, source_target_pairs={{0,4},{4,0},{1,5},{5,1},{2,6},{6,2},{3,7},{7,3},{8,12},{12,8},{9,1... | collective-permute-start | bytes 1572872 | tf_op jit(solution)/shard_map/ppermute | solution.py:658
  28.4 25.8 %collective-permute-start.2 = (bf16[2,64,2048]{2,1,0:T(8,128)(2,1)}, bf16[2,64,2048]{2,1,0:T(8,128)(2,1)S(1)}, u32[]{:S(2)}, u32[]{:S(2)}) collective-permute-start(bf16[2,64,2048]{2,1,0:T(8,128)(2,1)} %collective-permute-done), channel_id=1, source_target_pairs={{0,2},{1,3},{2,0},{3,1},{4,6},{5,7},{6,4},{7,5},{8,10},{9,11},{10,... | collective-permute-start | bytes 1572872 | tf_op jit(solution)/shard_map/ppermute | solution.py:722
  30.0 24.3 %collective-permute-start.3 = (bf16[2,64,2048]{2,1,0:T(8,128)(2,1)}, bf16[2,64,2048]{2,1,0:T(8,128)(2,1)S(1)}, u32[]{:S(2)}, u32[]{:S(2)}) collective-permute-start(bf16[2,64,2048]{2,1,0:T(8,128)(2,1)} %collective-permute-done), channel_id=1, source_target_pairs={{0,3},{1,2},{2,1},{3,0},{4,7},{5,6},{6,5},{7,4},{8,11},{9,10},{10,... | collective-permute-start | bytes 1572872 | tf_op jit(solution)/shard_map/ppermute | solution.py:722
  71.8 62.1 %all-to-all-start.1 = ((bf16[8,576,256]{2,1,0:T(8,128)(2,1)}), bf16[8,576,256]{2,1,0:T(8,128)(2,1)}, u32[]{:S(2)}, u32[]{:S(2)}) async-start(bf16[8,576,256]{2,1,0:T(8,128)(2,1)} %copy-done.6), calls=%async_computation.1 | async-start | bytes 4718592 | tf_op jit(solution)/shard_map/all_to_all | solution.py:654
  100.1 24.8 %collective-permute-start.13 = (bf16[2,64,2048]{2,1,0:T(8,128)(2,1)S(1)}, bf16[2,64,2048]{2,1,0:T(8,128)(2,1)S(1)}, u32[]{:S(2)}, u32[]{:S(2)}) collective-permute-start(bf16[2,64,2048]{2,1,0:T(8,128)(2,1)S(1)} %add_convert_fusion.5), channel_id=1, source_target_pairs={{0,2},{1,3},{2,0},{3,1},{4,6},{5,7},{6,4},{7,5},{8,10},{9,11},{10,... | collective-permute-start | bytes 1572872 | tf_op jit(solution)/shard_map/ppermute | solution.py:722
  100.8 24.2 %collective-permute-start.15 = (bf16[2,64,2048]{2,1,0:T(8,128)(2,1)S(1)}, bf16[2,64,2048]{2,1,0:T(8,128)(2,1)S(1)}, u32[]{:S(2)}, u32[]{:S(2)}) collective-permute-start(bf16[2,64,2048]{2,1,0:T(8,128)(2,1)S(1)} %add_convert_fusion.4), channel_id=1, source_target_pairs={{0,1},{1,0},{2,3},{3,2},{4,5},{5,4},{6,7},{7,6},{8,9},{9,8},{10,11... | collective-permute-start | bytes 1572872 | tf_op jit(solution)/shard_map/ppermute | solution.py:722
  147.4 42.3 %all-to-all-start.2 = ((bf16[8,256,384]{2,1,0:T(8,128)(2,1)}), bf16[8,256,384]{2,1,0:T(8,128)(2,1)}, u32[]{:S(2)}, u32[]{:S(2)}) async-start(bf16[8,256,384]{2,1,0:T(8,128)(2,1)} %get-tuple-element.107), calls=%async_computation.2 | async-start | bytes 3145728 | tf_op jit(solution)/shard_map/all_to_all | solution.py:654
  154.4 24.3 %collective-permute-start.21 = (bf16[2,64,2048]{2,1,0:T(8,128)(2,1)S(1)}, bf16[2,64,2048]{2,1,0:T(8,128)(2,1)S(1)}, u32[]{:S(2)}, u32[]{:S(2)}) collective-permute-start(bf16[2,64,2048]{2,1,0:T(8,128)(2,1)S(1)} %multiply_convert_fusion.1.refs_4_), channel_id=1, source_target_pairs={{0,2},{1,3},{2,0},{3,1},{4,6},{5,7},{6,4},{7,5},{8,10},{9,11},{10,... | collective-permute-start | bytes 1572872 | tf_op jit(solution)/shard_map/ppermute | solution.py:722
  155.9 24.4 %collective-permute-start.23 = (bf16[2,64,2048]{2,1,0:T(8,128)(2,1)S(1)}, bf16[2,64,2048]{2,1,0:T(8,128)(2,1)S(1)}, u32[]{:S(2)}, u32[]{:S(2)}) collective-permute-start(bf16[2,64,2048]{2,1,0:T(8,128)(2,1)S(1)} %multiply_convert_fusion.1.refs_4_), channel_id=1, source_target_pairs={{0,3},{1,2},{2,1},{3,0},{4,7},{5,6},{6,5},{7,4},{8,11},{9,10},{10,... | collective-permute-start | bytes 1572872 | tf_op jit(solution)/shard_map/ppermute | solution.py:722
  157.4 23.0 %collective-permute-start.18 = (bf16[2,64,2048]{2,1,0:T(8,128)(2,1)S(1)}, bf16[2,64,2048]{2,1,0:T(8,128)(2,1)S(1)}, u32[]{:S(2)}, u32[]{:S(2)}) collective-permute-start(bf16[2,64,2048]{2,1,0:T(8,128)(2,1)S(1)} %multiply_convert_fusion.1.refs_4_), channel_id=1, source_target_pairs={{0,4},{4,0},{1,5},{5,1},{2,6},{6,2},{3,7},{7,3},{8,12},{12,8},{9,1... | collective-permute-start | bytes 1572872 | tf_op jit(solution)/shard_map/ppermute | solution.py:658
  218.1 23.4 %collective-permute-start.32 = (bf16[2,64,2048]{2,1,0:T(8,128)(2,1)S(1)}, bf16[2,64,2048]{2,1,0:T(8,128)(2,1)S(1)}, u32[]{:S(2)}, u32[]{:S(2)}) collective-permute-start(bf16[2,64,2048]{2,1,0:T(8,128)(2,1)S(1)} %fusion.11), channel_id=1, source_target_pairs={{0,2},{1,3},{2,0},{3,1},{4,6},{5,7},{6,4},{7,5},{8,10},{9,11},{10,... | collective-permute-start | bytes 1572872 | tf_op jit(solution)/shard_map/ppermute | solution.py:722
  218.8 22.8 %collective-permute-start.33 = (bf16[2,64,2048]{2,1,0:T(8,128)(2,1)S(1)}, bf16[2,64,2048]{2,1,0:T(8,128)(2,1)S(1)}, u32[]{:S(2)}, u32[]{:S(2)}) collective-permute-start(bf16[2,64,2048]{2,1,0:T(8,128)(2,1)S(1)} %fusion.10), channel_id=1, source_target_pairs={{0,1},{1,0},{2,3},{3,2},{4,5},{5,4},{6,7},{7,6},{8,9},{9,8},{10,11... | collective-permute-start | bytes 1572872 | tf_op jit(solution)/shard_map/ppermute | solution.py:722
  257.8 74.4 %all-to-all-start.3 = ((bf16[8,256,640]{2,1,0:T(8,128)(2,1)}), bf16[8,256,640]{2,1,0:T(8,128)(2,1)S(1)}, u32[]{:S(2)}, u32[]{:S(2)}) async-start(bf16[8,256,640]{2,1,0:T(8,128)(2,1)} %bitcast.108), calls=%async_computation.3 | async-start | bytes 5242880 | tf_op jit(solution)/shard_map/all_to_all | solution.py:654
  264.6 26.4 %collective-permute-start.30 = (bf16[2,64,2048]{2,1,0:T(8,128)(2,1)}, bf16[2,64,2048]{2,1,0:T(8,128)(2,1)S(1)}, u32[]{:S(2)}, u32[]{:S(2)}) collective-permute-start(bf16[2,64,2048]{2,1,0:T(8,128)(2,1)} %copy-done.31), channel_id=1, source_target_pairs={{0,4},{4,0},{1,5},{5,1},{2,6},{6,2},{3,7},{7,3},{8,12},{12,8},{9,1... | collective-permute-start | bytes 1572872 | tf_op jit(solution)/shard_map/ppermute | solution.py:658
  264.9 25.6 %collective-permute-start.36 = (bf16[2,64,2048]{2,1,0:T(8,128)(2,1)}, bf16[2,64,2048]{2,1,0:T(8,128)(2,1)S(1)}, u32[]{:S(2)}, u32[]{:S(2)}) collective-permute-start(bf16[2,64,2048]{2,1,0:T(8,128)(2,1)} %get-tuple-element.170.refs_4_), channel_id=1, source_target_pairs={{0,2},{1,3},{2,0},{3,1},{4,6},{5,7},{6,4},{7,5},{8,10},{9,11},{10,... | collective-permute-start | bytes 1572872 | tf_op jit(solution)/shard_map/ppermute | solution.py:722
  266.4 24.1 %collective-permute-start.37 = (bf16[2,64,2048]{2,1,0:T(8,128)(2,1)}, bf16[2,64,2048]{2,1,0:T(8,128)(2,1)S(1)}, u32[]{:S(2)}, u32[]{:S(2)}) collective-permute-start(bf16[2,64,2048]{2,1,0:T(8,128)(2,1)} %get-tuple-element.170.refs_4_), channel_id=1, source_target_pairs={{0,3},{1,2},{2,1},{3,0},{4,7},{5,6},{6,5},{7,4},{8,11},{9,10},{10,... | collective-permute-start | bytes 1572872 | tf_op jit(solution)/shard_map/ppermute | solution.py:722
  269.1 23.6 %collective-permute-start.43 = (bf16[2,64,2048]{2,1,0:T(8,128)(2,1)}, bf16[2,64,2048]{2,1,0:T(8,128)(2,1)S(1)}, u32[]{:S(2)}, u32[]{:S(2)}) collective-permute-start(bf16[2,64,2048]{2,1,0:T(8,128)(2,1)} %get-tuple-element.170.refs_4_), channel_id=1, source_target_pairs={{0,4},{4,0},{1,5},{5,1},{2,6},{6,2},{3,7},{7,3},{8,12},{12,8},{9,1... | collective-permute-start | bytes 1572872 | tf_op jit(solution)/shard_map/ppermute | solution.py:658
  292.7 24.8 %collective-permute-start.40 = (bf16[2,64,2048]{2,1,0:T(8,128)(2,1)S(1)}, bf16[2,64,2048]{2,1,0:T(8,128)(2,1)S(1)}, u32[]{:S(2)}, u32[]{:S(2)}) collective-permute-start(bf16[2,64,2048]{2,1,0:T(8,128)(2,1)S(1)} %convert_add_fusion.4), channel_id=1, source_target_pairs={{0,2},{1,3},{2,0},{3,1},{4,6},{5,7},{6,4},{7,5},{8,10},{9,11},{10,... | collective-permute-start | bytes 1572872 | tf_op jit(solution)/shard_map/ppermute | solution.py:722
  294.2 23.3 %collective-permute-start.38 = (bf16[2,64,2048]{2,1,0:T(8,128)(2,1)S(1)}, bf16[2,64,2048]{2,1,0:T(8,128)(2,1)S(1)}, u32[]{:S(2)}, u32[]{:S(2)}) collective-permute-start(bf16[2,64,2048]{2,1,0:T(8,128)(2,1)S(1)} %convert_add_fusion.6), channel_id=1, source_target_pairs={{0,3},{1,2},{2,1},{3,0},{4,7},{5,6},{6,5},{7,4},{8,11},{9,10},{10,... | collective-permute-start | bytes 1572872 | tf_op jit(solution)/shard_map/ppermute | solution.py:722
  295.9 28.7 %collective-permute-start.29 = (bf16[2,64,2048]{2,1,0:T(8,128)(2,1)S(1)}, bf16[2,64,2048]{2,1,0:T(8,128)(2,1)S(1)}, u32[]{:S(2)}, u32[]{:S(2)}) collective-permute-start(bf16[2,64,2048]{2,1,0:T(8,128)(2,1)S(1)} %copy-done.30), channel_id=1, source_target_pairs={{0,4},{4,0},{1,5},{5,1},{2,6},{6,2},{3,7},{7,3},{8,12},{12,8},{9,1... | collective-permute-start | bytes 1572872 | tf_op jit(solution)/shard_map/ppermute | solution.py:658
  332.2 44.3 %all-to-all-start.4 = ((bf16[8,264,384]{2,1,0:T(8,128)(2,1)}), bf16[8,264,384]{2,1,0:T(8,128)(2,1)}, u32[]{:S(2)}, u32[]{:S(2)}) async-start(bf16[8,264,384]{2,1,0:T(8,128)(2,1)} %fusion.6), calls=%async_computation.4 | async-start | bytes 3244032 | tf_op jit(solution)/shard_map/all_to_all | solution.py:654
  382.1 47.1 %all-to-all-start.5 = ((bf16[8,448,256]{2,1,0:T(8,128)(2,1)}), bf16[8,448,256]{2,1,0:T(8,128)(2,1)S(1)}, u32[]{:S(2)}, u32[]{:S(2)}) async-start(bf16[8,448,256]{2,1,0:T(8,128)(2,1)} %pad_maximum_fusion), calls=%async_computation.5 | async-start | bytes 3670016 | tf_op jit(solution)/shard_map/all_to_all | solution.py:654
  (116 other events, 1160.7 us)
where the time goes:
time: 438 us; the launch traced here: 432 us
  waiting for transfers between devices  204 us (47%)
  Pallas kernels  71.2 us (16%)
  starting transfers between devices  70.7 us (16%)
  other arithmetic  39.9 us (9%)
  local copies, waits for them, and re-layouts  33.6 us (8%)
  matrix products  10.1 us (2%)
    ppermute x27, waiting for transfers between devices, shifted(): return lax.ppermute(block, 'mp', [(i, i ^ away) for i in range(mp_count)])  128 us
    ppermute x34, waiting for transfers between devices, swap(): return lax.ppermute(block, axis, [(0, 1), (1, 0)])  42.4 us
    all_to_all x6, waiting for transfers between devices, exchange(): return lax.all_to_all(blocks, axes, split_axis=0, concat_axis=0, tiled=True)  33.6 us
    ppermute x27, starting transfers between devices, shifted(): return lax.ppermute(block, 'mp', [(i, i ^ away) for i in range(mp_count)])  32.3 us
    all_to_all x6, starting transfers between devices, exchange(): return lax.all_to_all(blocks, axes, split_axis=0, concat_axis=0, tiled=True)  29.3 us
    pallas_call x1, Pallas kernels, feed_forward(): pl.pallas_call(functools.partial(ffn_kernel, near_count, count), grid=(CO...  19.9 us
    pallas_call x1, Pallas kernels, attention_backward(): pl.pallas_call(functools.partial(backward_kernel, heads, shard, near_coun...  15 us
    unnamed x146, local copies, waits for them, and re-layouts  12.9 us
  transfers between devices with their start and end apart: 67, of which 36 were waited for; matrix products, arithmetic and copies ran while one was open for 15% of the time, Pallas kernels for 12%

commit v1 on v0

--- a/solution.py
+++ b/solution.py
@@ -726,17 +726,19 @@
             [jnp.where(near_at == 0, own, moved), jnp.where(near_at == 0, moved, own)], 0
         )
 
-    def near_rows(blocks):
+    def near_rows(blocks, meanwhile):
         own = [lax.dynamic_slice_in_dim(block, mp_at * own_rows, own_rows, 0) for block in blocks]
         near = swap(jnp.stack(own), "near")
         came = [(0, near)] + [(away, shifted(near, away)) for away in range(1, mp_count)]
+        made = meanwhile(came[1][1])
+        came = came[:2] + [(away, after(block, *made)) for away, block in came[2:]]
         halves = []
         for half in (came, [(away, swap(block, "core")) for away, block in came]):
             rows = jnp.zeros((len(blocks), mp_count, own_rows, model), near.dtype)
             for away, block in half:
                 rows = lax.dynamic_update_index_in_dim(rows, block, mp_at ^ away, 1)
             halves.append([rows[i].reshape(tok_rows, model) for i in range(len(blocks))])
-        return *halves, came[1][1]
+        return *halves, made
 
     def in_order(own, moved, core, core_moved):
         rows = jnp.zeros((CORES, near_count, tok_rows, model), own.dtype)
@@ -796,13 +798,17 @@
         values = rows.astype(F32)
         return (values * rms(values)).astype(LOW)
 
-    (moved_inputs, moved_cotangent), core_moved, first_came = near_rows([inputs, cotangent])
+    def make_blocks(first_came):
+        return ffn_blocks(
+            w_gate, w_up, w_down, after(ffn_scale.reshape(1, shard), first_came), seqs, members
+        )
+
+    (moved_inputs, moved_cotangent), core_moved, (ffn_first, ffn_second) = near_rows(
+        [inputs, cotangent], make_blocks
+    )
     input_parts = [inputs, moved_inputs, swap(inputs, "core"), core_moved[0]]
     core_cotangent = swap(after(cotangent, moved_inputs), "core")
     grad_parts = [cotangent, moved_cotangent, core_cotangent, core_moved[1]]
-    ffn_first, ffn_second = ffn_blocks(
-        w_gate, w_up, w_down, after(ffn_scale.reshape(1, shard), first_came), seqs, members
-    )
     parts = [normed(part) for part in input_parts]
     parts = lax.optimization_barrier((*parts, ffn_first, ffn_second))[:4]
     first_got = exchange(after(ffn_first, attn_got), COLUMN)
@@ -860,19 +866,20 @@
     )
     qkv_product = functools.partial(column_product, shard, 0, 3 * width)
     ffn_moved = send_mp([after(rows, *mine_one[1:]) for rows in ffn_cores])
-    inner_cores = sum_cores(
-        *partial(after(d_qkv, *ffn_moved), attn_got, qkv_product, "attention_in")
-    )
-    inner_pair = sum_mp(inner_cores)
     table_sent = d_table[:, :heads].astype(LOW).reshape(sources, table_rows, heads)
     table_sent = jnp.pad(
         table_sent, ((0, 0), (0, EXTRA - table_rows), (0, 3 * width - heads))
     )
     d_qkv_w = contract_rows(normed_rows, d_qkv).astype(LOW).reshape(sources, shard, -1)
     d_qkv_sent = jnp.concatenate([d_qkv_w, table_sent], 1)
+    inner_cores = sum_cores(
+        *partial(after(d_qkv, d_qkv_sent, *ffn_moved), attn_got, qkv_product, "attention_in")
+    )
+    inner_pair = sum_mp(inner_cores)
     d_qkv_got = to_owners(after(d_qkv_sent, d_gate_up))
     d_out = contract_rows(after(attended, inner_cores[0]), rows_one)
     d_out = jnp.moveaxis(d_out.astype(LOW).reshape(width, sources, shard), 1, 0)
+    d_rows_sent = jnp.concatenate([d_down_w, d_out], 1)
 
     (d_w_gate, d_w_up), ffn_gain, _ = owner_grads(
         after(d_gate_up, inner_cores[0]), (w_gate, w_up), ffn_scale.reshape(1, shard), members, None
@@ -882,7 +889,7 @@
     )
     inner_sent, inner_kept = split_near(inner_pair)
     came = swap(
-        after(jnp.stack([ffn_sent, inner_sent]), d_qkv_got, ffn_gain), "near"
+        after(jnp.stack([ffn_sent, inner_sent]), d_qkv_got, ffn_gain, d_rows_sent), "near"
     )
     own_inputs = here(pair_inputs)
     inv_one = rms(own_inputs)
@@ -891,7 +898,7 @@
     owned = jnp.stack([own_out.astype(LOW), grad_input.astype(LOW)])
     rows_out = [jnp.zeros((mp_count, own_rows, model), LOW)] * 2
     blocks_out = [owned] + [shifted(owned, away) for away in range(1, mp_count)]
-    d_rows = to_owners(after(jnp.concatenate([d_down_w, d_out], 1), d_qkv_got))
+    d_rows = to_owners(after(d_rows_sent, d_qkv_got))
     for away, block in enumerate(blocks_out):
         rows_out = [
             lax.dynamic_update_index_in_dim(rows, block[i], mp_at ^ away, 0)

time: 438 us -> 429 us (0.979)
  waiting for transfers between devices: 204 us -> 183 us
  local copies, waits for them, and re-layouts: 33.6 us -> 44.9 us
    ppermute x27, waiting for transfers between devices: 128 us -> 106 us  [shifted(): return lax.ppermute(block, 'mp', [(i, i ^ away) for i in range(mp_count)])]
    ppermute x34, waiting for transfers between devices: 42.4 us -> 47 us  [swap(): return lax.ppermute(block, axis, [(0, 1), (1, 0)])]
    unnamed x146 -> x144, local copies, waits for them, and re-layouts: 12.9 us -> 15.3 us
  transfers between devices with their start and end apart: 67 -> 67, of which waited for: 36 -> 35; matrix products, arithmetic and copies ran while one was open for 15% -> 17% of each run, Pallas kernels for 12% -> 12%
where the time goes in v1:
time: 429 us; the launch traced here: 422 us
  waiting for transfers between devices  183 us (43%)
  Pallas kernels  72 us (17%)
  starting transfers between devices  71.1 us (17%)
  local copies, waits for them, and re-layouts  44.9 us (10%)
  other arithmetic  39.3 us (9%)
  matrix products  10.1 us (2%)
    ppermute x27, waiting for transfers between devices, shifted(): return lax.ppermute(block, 'mp', [(i, i ^ away) for i in range(mp_count)])  106 us
    ppermute x34, waiting for transfers between devices, swap(): return lax.ppermute(block, axis, [(0, 1), (1, 0)])  47 us
    ppermute x27, starting transfers between devices, shifted(): return lax.ppermute(block, 'mp', [(i, i ^ away) for i in range(mp_count)])  32 us
    all_to_all x6, waiting for transfers between devices, exchange(): return lax.all_to_all(blocks, axes, split_axis=0, concat_axis=0, tiled=True)  30 us
    all_to_all x6, starting transfers between devices, exchange(): return lax.all_to_all(blocks, axes, split_axis=0, concat_axis=0, tiled=True)  29.7 us
    pallas_call x1, Pallas kernels, feed_forward(): pl.pallas_call(functools.partial(ffn_kernel, near_count, count), grid=(CO...  19.8 us
    unnamed x144, local copies, waits for them, and re-layouts  15.3 us
    pallas_call x1, Pallas kernels, attention_backward(): pl.pallas_call(functools.partial(backward_kernel, heads, shard, near_coun...  15.1 us
  transfers between devices with their start and end apart: 67, of which 35 were waited for; matrix products, arithmetic and copies ran while one was open for 17% of the time, Pallas kernels for 12%

profile of v1, /device:TPU:0, one launch (start us, length us, event | category | flops | bytes accessed | tf_op | source)
XLA Modules:
  0.0 422.4 jit_solution(4233292177564633077)
XLA Ops:
  14.1 6.0 %collective-permute-done = bf16[2,64,2048]{2,1,0:T(8,128)(2,1)} collective-permute-done((bf16[2,64,2048]{2,1,0:T(8,128)(2,1)S(1)}, bf16[2,64,2048]{2,1,0:T(8,128)(2,1)}, u32[]{:S(2)}, u32[]{:S(2)}) %collective-permute-start) | collective-permute-done | bytes 524320 | tf_op jit(solution)/shard_map/ppermute | solution.py:658
  38.5 7.5 %collective-permute-done.2 = bf16[2,64,2048]{2,1,0:T(8,128)(2,1)} collective-permute-done((bf16[2,64,2048]{2,1,0:T(8,128)(2,1)}, bf16[2,64,2048]{2,1,0:T(8,128)(2,1)}, u32[]{:S(2)}, u32[]{:S(2)}) %collective-permute-start.2) | collective-permute-done | bytes 524320 | tf_op jit(solution)/shard_map/ppermute | solution.py:722
  66.9 7.2 %all-to-all-start.1 = ((bf16[8,576,256]{2,1,0:T(8,128)(2,1)}), bf16[8,576,256]{2,1,0:T(8,128)(2,1)}, u32[]{:S(2)}, u32[]{:S(2)}) async-start(bf16[8,576,256]{2,1,0:T(8,128)(2,1)} %copy-done.6), calls=%async_computation.1 | async-start | bytes 4718592 | tf_op jit(solution)/shard_map/all_to_all | solution.py:654
  78.0 11.8 %attention_forward.1 = (bf16[1024,384]{1,0:T(8,128)(2,1)S(1)}, bf16[1024,128]{1,0:T(8,128)(2,1)S(1)}, bf16[2,1024,1024]{2,1,0:T(8,128)(2,1)S(1)}, bf16[2,64,2048...) custom-call(s32[5]{0:T(128)S(1)} %stack.62.place_ref, ...), custom_call_target="tpu_custom_call" | custom-call | tf_op jit(solution)/shard_map/attention_forward/pallas_call | solution.py:146
  100.6 8.5 %collective-permute-done.11 = bf16[2,64,2048]{2,1,0:T(8,128)(2,1)S(1)} collective-permute-done((bf16[2,64,2048]{2,1,0:T(8,128)(2,1)S(1)}, bf16[2,64,2048]{2,1,0:T(8,128)(2,1)S(1)}, u32[]{:S(2)}, u32[]{:S(2)}) %collective-permute-start.11) | collective-permute-done | bytes 524320 | tf_op jit(solution)/shard_map/ppermute | solution.py:722
  109.1 10.8 %collective-permute-done.13 = bf16[2,64,2048]{2,1,0:T(8,128)(2,1)S(1)} collective-permute-done((bf16[2,64,2048]{2,1,0:T(8,128)(2,1)S(1)}, bf16[2,64,2048]{2,1,0:T(8,128)(2,1)S(1)}, u32[]{:S(2)}, u32[]{:S(2)}) %collective-permute-start.13) | collective-permute-done | bytes 524320 | tf_op jit(solution)/shard_map/ppermute | solution.py:722
  120.5 8.4 %all-to-all-done.1.refs_9_.weight_ref = bf16[8,576,256]{2,1,0:T(8,128)(2,1)} async-done(((bf16[8,576,256]{2,1,0:T(8,128)(2,1)}), bf16[8,576,256]{2,1,0:T(8,128)(2,1)}, u32[]{:S(2)}, u32[]{:S(2)}) %all-to-all-start.1) | async-done | bytes 2359328 | tf_op jit(solution)/shard_map/all_to_all | solution.py:654
  128.9 13.5 %collective-permute-done.17 = bf16[2,64,2048]{2,1,0:T(8,128)(2,1)S(1)} collective-permute-done((bf16[2,64,2048]{2,1,0:T(8,128)(2,1)S(1)}, bf16[2,64,2048]{2,1,0:T(8,128)(2,1)S(1)}, u32[]{:S(2)}, u32[]{:S(2)}) %collective-permute-start.17) | collective-permute-done | bytes 524320 | tf_op jit(solution)/shard_map/ppermute | solution.py:658
  152.3 11.2 %collective-permute-done.19.refs_5_ = bf16[2,64,2048]{2,1,0:T(8,128)(2,1)S(1)} collective-permute-done((bf16[2,64,2048]{2,1,0:T(8,128)(2,1)S(1)}, bf16[2,64,2048]{2,1,0:T(8,128)(2,1)S(1)}, u32[]{:S(2)}, u32[]{:S(2)}) %collective-permute-start.19) | collective-permute-done | bytes 524320 | tf_op jit(solution)/shard_map/ppermute | solution.py:722
  163.5 10.1 %collective-permute-done.21.refs_6_ = bf16[2,64,2048]{2,1,0:T(8,128)(2,1)S(1)} collective-permute-done((bf16[2,64,2048]{2,1,0:T(8,128)(2,1)S(1)}, bf16[2,64,2048]{2,1,0:T(8,128)(2,1)S(1)}, u32[]{:S(2)}, u32[]{:S(2)}) %collective-permute-start.21) | collective-permute-done | bytes 524320 | tf_op jit(solution)/shard_map/ppermute | solution.py:722
  177.3 7.4 %all-to-all-done.2.refs_10_ = bf16[8,256,384]{2,1,0:T(8,128)(2,1)} async-done(((bf16[8,256,384]{2,1,0:T(8,128)(2,1)}), bf16[8,256,384]{2,1,0:T(8,128)(2,1)}, u32[]{:S(2)}, u32[]{:S(2)}) %all-to-all-start.2) | async-done | bytes 1572896 | tf_op jit(solution)/shard_map/all_to_all | solution.py:654
  184.7 19.8 %feed_forward.1 = (bf16[2,64,2048]{2,1,0:T(8,128)(2,1)}, bf16[2,64,2048]{2,1,0:T(8,128)(2,1)}, bf16[2,64,2048]{2,1,0:T(8,128)(2,1)}, bf16[2,64,2048]{2,1,0:T(8,1...) custom-call(s32[5]{0:T(128)} %copy-done.23, ...), custom_call_target="tpu_custom_call" | custom-call | flops 8053063680 | bytes 25165824 | tf_op jit(solution)/shard_map/feed_forward/pallas_call | solution.py:616
  215.2 5.8 %ffn_out.1 = (bf16[2,64,2048]{2,1,0:T(8,128)(2,1)S(1)}, bf16[2,64,2048]{2,1,0:T(8,128)(2,1)}, bf16[2,64,2048]{2,1,0:T(8,128)(2,1)S(1)}, bf16[2,64,2048]{2,1,0:T(...) custom-call(s32[5]{0:T(128)S(1)} %copy-done.24, ...), custom_call_target="tpu_custom_call" | custom-call | flops 1342177280 | bytes 4194304 | tf_op jit(solution)/shard_map/ffn_out/pallas_call | solution.py:480
  226.0 10.4 %collective-permute-done.32 = bf16[2,64,2048]{2,1,0:T(8,128)(2,1)S(1)} collective-permute-done((bf16[2,64,2048]{2,1,0:T(8,128)(2,1)S(1)}, bf16[2,64,2048]{2,1,0:T(8,128)(2,1)S(1)}, u32[]{:S(2)}, u32[]{:S(2)}) %collective-permute-start.32) | collective-permute-done | bytes 524320 | tf_op jit(solution)/shard_map/ppermute | solution.py:722
  238.9 11.8 %collective-permute-done.34 = bf16[2,64,2048]{2,1,0:T(8,128)(2,1)S(1)} collective-permute-done((bf16[2,64,2048]{2,1,0:T(8,128)(2,1)S(1)}, bf16[2,64,2048]{2,1,0:T(8,128)(2,1)S(1)}, u32[]{:S(2)}, u32[]{:S(2)}) %collective-permute-start.34) | collective-permute-done | bytes 524320 | tf_op jit(solution)/shard_map/ppermute | solution.py:658
  262.9 9.0 %collective-permute-done.35.refs_5_ = bf16[2,64,2048]{2,1,0:T(8,128)(2,1)S(1)} collective-permute-done((bf16[2,64,2048]{2,1,0:T(8,128)(2,1)}, bf16[2,64,2048]{2,1,0:T(8,128)(2,1)S(1)}, u32[]{:S(2)}, u32[]{:S(2)}) %collective-permute-start.35) | collective-permute-done | bytes 524320 | tf_op jit(solution)/shard_map/ppermute | solution.py:722
  271.9 9.8 %collective-permute-done.36.refs_6_ = bf16[2,64,2048]{2,1,0:T(8,128)(2,1)S(1)} collective-permute-done((bf16[2,64,2048]{2,1,0:T(8,128)(2,1)}, bf16[2,64,2048]{2,1,0:T(8,128)(2,1)S(1)}, u32[]{:S(2)}, u32[]{:S(2)}) %collective-permute-start.36) | collective-permute-done | bytes 524320 | tf_op jit(solution)/shard_map/ppermute | solution.py:722
  290.9 15.1 %attention_backward.1 = (bf16[1024,384]{1,0:T(8,128)(2,1)S(1)}, f32[32,128]{1,0:T(8,128)S(1)}, bf16[1024,2048]{1,0:T(8,128)(2,1)S(1)}) custom-call(s32[5]{0:T(128)S(1)} %copy-done.24, bf16[2,64,2048]{2,1,0:T(8,128)(2,1)S(1)} %collective-permute-done.43.refs_0_, bf16[2,64,2048]{2,1,0:T(8,128)(2,1)S(1)} %collective-permute-done.44.refs_1_, ...), custom_call_target="tpu_custom_call" | custom-call | flops 4294967296 | bytes 4194304 | tf_op jit(solution)/shard_map/attention_backward/pallas_call | solution.py:256
  311.3 5.9 %attention_in.1 = (bf16[2,64,2048]{2,1,0:T(8,128)(2,1)}, bf16[2,64,2048]{2,1,0:T(8,128)(2,1)}, bf16[2,64,2048]{2,1,0:T(8,128)(2,1)}, bf16[2,64,2048]{2,1,0:T(8,1...) custom-call(s32[5]{0:T(128)S(1)} %copy-done.24, ...), custom_call_target="tpu_custom_call" | custom-call | flops 1610612736 | bytes 4194304 | tf_op jit(solution)/shard_map/attention_in/pallas_call | solution.py:480
  323.1 5.4 %all-to-all-start.4 = ((bf16[8,264,384]{2,1,0:T(8,128)(2,1)}), bf16[8,264,384]{2,1,0:T(8,128)(2,1)}, u32[]{:S(2)}, u32[]{:S(2)}) async-start(bf16[8,264,384]{2,1,0:T(8,128)(2,1)} %fusion.6), calls=%async_computation.4 | async-start | bytes 3244032 | tf_op jit(solution)/shard_map/all_to_all | solution.py:654
  342.5 5.5 %collective-permute-done.51 = bf16[2,64,2048]{2,1,0:T(8,128)(2,1)} collective-permute-done((bf16[2,64,2048]{2,1,0:T(8,128)(2,1)}, bf16[2,64,2048]{2,1,0:T(8,128)(2,1)}, u32[]{:S(2)}, u32[]{:S(2)}) %collective-permute-start.51) | collective-permute-done | bytes 524320 | tf_op jit(solution)/shard_map/ppermute | solution.py:722
  356.6 10.8 %all-to-all-done.4.refs_0_.refs_1_ = bf16[8,264,384]{2,1,0:T(8,128)(2,1)} async-done(((bf16[8,264,384]{2,1,0:T(8,128)(2,1)}), bf16[8,264,384]{2,1,0:T(8,128)(2,1)}, u32[]{:S(2)}, u32[]{:S(2)}) %all-to-all-start.4) | async-done | bytes 1622048 | tf_op jit(solution)/shard_map/all_to_all | solution.py:654
  374.1 10.8 %collective-permute-done.54 = bf16[2,64,2048]{2,1,0:T(8,128)(2,1)S(1)} collective-permute-done((bf16[2,64,2048]{2,1,0:T(8,128)(2,1)}, bf16[2,64,2048]{2,1,0:T(8,128)(2,1)S(1)}, u32[]{:S(2)}, u32[]{:S(2)}) %collective-permute-start.54) | collective-permute-done | bytes 524320 | tf_op jit(solution)/shard_map/ppermute | solution.py:658
  391.6 11.4 %collective-permute-done.55 = bf16[2,64,2048]{2,1,0:T(8,128)(2,1)S(1)} collective-permute-done((bf16[2,64,2048]{2,1,0:T(8,128)(2,1)S(1)}, bf16[2,64,2048]{2,1,0:T(8,128)(2,1)S(1)}, u32[]{:S(2)}, u32[]{:S(2)}) %collective-permute-start.55) | collective-permute-done | bytes 524320 | tf_op jit(solution)/shard_map/ppermute | solution.py:722
  (363 shorter events, 186.5 us)
Async XLA Ops:
  0.6 51.8 %collective-permute-start.4 = (bf16[256,2048]{1,0:T(8,128)(2,1)}, bf16[256,2048]{1,0:T(8,128)(2,1)}, u32[]{:S(2)}, u32[]{:S(2)}) collective-permute-start(bf16[256,2048]{1,0:T(8,128)(2,1)} %param.13), channel_id=1, source_target_pairs={{0,4},{4,0},{1,5},{5,1},{2,6},{6,2},{3,7},{7,3},{8,12},{12,8},{9,1... | collective-permute-start | bytes 3145736 | tf_op jit(solution)/shard_map/ppermute | solution.py:658
  9.1 57.9 %all-to-all-start = ((bf16[8,264,512]{2,1,0:T(8,128)(2,1)}), bf16[8,264,512]{2,1,0:T(8,128)(2,1)}, u32[]{:S(2)}, u32[]{:S(2)}) async-start(bf16[8,264,512]{2,1,0:T(8,128)(2,1)} %attention_blocks.1), calls=%async_computation | async-start | bytes 4325376 | tf_op jit(solution)/shard_map/all_to_all | solution.py:654
  22.2 23.8 %collective-permute-start.2 = (bf16[2,64,2048]{2,1,0:T(8,128)(2,1)}, bf16[2,64,2048]{2,1,0:T(8,128)(2,1)}, u32[]{:S(2)}, u32[]{:S(2)}) collective-permute-start(bf16[2,64,2048]{2,1,0:T(8,128)(2,1)} %collective-permute-done), channel_id=1, source_target_pairs={{0,2},{1,3},{2,0},{3,1},{4,6},{5,7},{6,4},{7,5},{8,10},{9,11},{10,... | collective-permute-start | bytes 1572872 | tf_op jit(solution)/shard_map/ppermute | solution.py:722
  29.9 27.7 %collective-permute-start.5 = (bf16[2,64,2048]{2,1,0:T(8,128)(2,1)}, bf16[2,64,2048]{2,1,0:T(8,128)(2,1)}, u32[]{:S(2)}, u32[]{:S(2)}) collective-permute-start(bf16[2,64,2048]{2,1,0:T(8,128)(2,1)} %collective-permute-done), channel_id=1, source_target_pairs={{0,4},{4,0},{1,5},{5,1},{2,6},{6,2},{3,7},{7,3},{8,12},{12,8},{9,1... | collective-permute-start | bytes 1572872 | tf_op jit(solution)/shard_map/ppermute | solution.py:658
  66.9 61.9 %all-to-all-start.1 = ((bf16[8,576,256]{2,1,0:T(8,128)(2,1)}), bf16[8,576,256]{2,1,0:T(8,128)(2,1)}, u32[]{:S(2)}, u32[]{:S(2)}) async-start(bf16[8,576,256]{2,1,0:T(8,128)(2,1)} %copy-done.6), calls=%async_computation.1 | async-start | bytes 4718592 | tf_op jit(solution)/shard_map/all_to_all | solution.py:654
  95.1 24.8 %collective-permute-start.13 = (bf16[2,64,2048]{2,1,0:T(8,128)(2,1)S(1)}, bf16[2,64,2048]{2,1,0:T(8,128)(2,1)S(1)}, u32[]{:S(2)}, u32[]{:S(2)}) collective-permute-start(bf16[2,64,2048]{2,1,0:T(8,128)(2,1)S(1)} %add_convert_fusion.5), channel_id=1, source_target_pairs={{0,2},{1,3},{2,0},{3,1},{4,6},{5,7},{6,4},{7,5},{8,10},{9,11},{10,... | collective-permute-start | bytes 1572872 | tf_op jit(solution)/shard_map/ppermute | solution.py:722
  96.1 23.9 %collective-permute-start.15 = (bf16[2,64,2048]{2,1,0:T(8,128)(2,1)S(1)}, bf16[2,64,2048]{2,1,0:T(8,128)(2,1)S(1)}, u32[]{:S(2)}, u32[]{:S(2)}) collective-permute-start(bf16[2,64,2048]{2,1,0:T(8,128)(2,1)S(1)} %add_convert_fusion.4), channel_id=1, source_target_pairs={{0,1},{1,0},{2,3},{3,2},{4,5},{5,4},{6,7},{7,6},{8,9},{9,8},{10,11... | collective-permute-start | bytes 1572872 | tf_op jit(solution)/shard_map/ppermute | solution.py:722
  142.4 42.3 %all-to-all-start.2 = ((bf16[8,256,384]{2,1,0:T(8,128)(2,1)}), bf16[8,256,384]{2,1,0:T(8,128)(2,1)}, u32[]{:S(2)}, u32[]{:S(2)}) async-start(bf16[8,256,384]{2,1,0:T(8,128)(2,1)} %get-tuple-element.111), calls=%async_computation.2 | async-start | bytes 3145728 | tf_op jit(solution)/shard_map/all_to_all | solution.py:654
  149.6 24.0 %collective-permute-start.21 = (bf16[2,64,2048]{2,1,0:T(8,128)(2,1)S(1)}, bf16[2,64,2048]{2,1,0:T(8,128)(2,1)S(1)}, u32[]{:S(2)}, u32[]{:S(2)}) collective-permute-start(bf16[2,64,2048]{2,1,0:T(8,128)(2,1)S(1)} %multiply_convert_fusion.1.refs_4_), channel_id=1, source_target_pairs={{0,2},{1,3},{2,0},{3,1},{4,6},{5,7},{6,4},{7,5},{8,10},{9,11},{10,... | collective-permute-start | bytes 1572872 | tf_op jit(solution)/shard_map/ppermute | solution.py:722
  150.8 24.4 %collective-permute-start.23 = (bf16[2,64,2048]{2,1,0:T(8,128)(2,1)S(1)}, bf16[2,64,2048]{2,1,0:T(8,128)(2,1)S(1)}, u32[]{:S(2)}, u32[]{:S(2)}) collective-permute-start(bf16[2,64,2048]{2,1,0:T(8,128)(2,1)S(1)} %multiply_convert_fusion.1.refs_4_), channel_id=1, source_target_pairs={{0,3},{1,2},{2,1},{3,0},{4,7},{5,6},{6,5},{7,4},{8,11},{9,10},{10,... | collective-permute-start | bytes 1572872 | tf_op jit(solution)/shard_map/ppermute | solution.py:722
  152.3 23.0 %collective-permute-start.18 = (bf16[2,64,2048]{2,1,0:T(8,128)(2,1)S(1)}, bf16[2,64,2048]{2,1,0:T(8,128)(2,1)S(1)}, u32[]{:S(2)}, u32[]{:S(2)}) collective-permute-start(bf16[2,64,2048]{2,1,0:T(8,128)(2,1)S(1)} %multiply_convert_fusion.1.refs_4_), channel_id=1, source_target_pairs={{0,4},{4,0},{1,5},{5,1},{2,6},{6,2},{3,7},{7,3},{8,12},{12,8},{9,1... | collective-permute-start | bytes 1572872 | tf_op jit(solution)/shard_map/ppermute | solution.py:658
  212.9 23.4 %collective-permute-start.32 = (bf16[2,64,2048]{2,1,0:T(8,128)(2,1)S(1)}, bf16[2,64,2048]{2,1,0:T(8,128)(2,1)S(1)}, u32[]{:S(2)}, u32[]{:S(2)}) collective-permute-start(bf16[2,64,2048]{2,1,0:T(8,128)(2,1)S(1)} %fusion.11), channel_id=1, source_target_pairs={{0,2},{1,3},{2,0},{3,1},{4,6},{5,7},{6,4},{7,5},{8,10},{9,11},{10,... | collective-permute-start | bytes 1572872 | tf_op jit(solution)/shard_map/ppermute | solution.py:722
  214.0 22.5 %collective-permute-start.33 = (bf16[2,64,2048]{2,1,0:T(8,128)(2,1)S(1)}, bf16[2,64,2048]{2,1,0:T(8,128)(2,1)S(1)}, u32[]{:S(2)}, u32[]{:S(2)}) collective-permute-start(bf16[2,64,2048]{2,1,0:T(8,128)(2,1)S(1)} %fusion.10), channel_id=1, source_target_pairs={{0,1},{1,0},{2,3},{3,2},{4,5},{5,4},{6,7},{7,6},{8,9},{9,8},{10,11... | collective-permute-start | bytes 1572872 | tf_op jit(solution)/shard_map/ppermute | solution.py:722
  252.6 70.5 %all-to-all-start.3 = ((bf16[8,256,640]{2,1,0:T(8,128)(2,1)}), bf16[8,256,640]{2,1,0:T(8,128)(2,1)S(1)}, u32[]{:S(2)}, u32[]{:S(2)}) async-start(bf16[8,256,640]{2,1,0:T(8,128)(2,1)} %bitcast.108), calls=%async_computation.3 | async-start | bytes 5242880 | tf_op jit(solution)/shard_map/all_to_all | solution.py:654
  257.8 23.9 %collective-permute-start.36 = (bf16[2,64,2048]{2,1,0:T(8,128)(2,1)}, bf16[2,64,2048]{2,1,0:T(8,128)(2,1)S(1)}, u32[]{:S(2)}, u32[]{:S(2)}) collective-permute-start(bf16[2,64,2048]{2,1,0:T(8,128)(2,1)} %get-tuple-element.174.refs_4_), channel_id=1, source_target_pairs={{0,2},{1,3},{2,0},{3,1},{4,6},{5,7},{6,4},{7,5},{8,10},{9,11},{10,... | collective-permute-start | bytes 1572872 | tf_op jit(solution)/shard_map/ppermute | solution.py:722
  259.0 24.3 %collective-permute-start.37 = (bf16[2,64,2048]{2,1,0:T(8,128)(2,1)}, bf16[2,64,2048]{2,1,0:T(8,128)(2,1)S(1)}, u32[]{:S(2)}, u32[]{:S(2)}) collective-permute-start(bf16[2,64,2048]{2,1,0:T(8,128)(2,1)} %get-tuple-element.174.refs_4_), channel_id=1, source_target_pairs={{0,3},{1,2},{2,1},{3,0},{4,7},{5,6},{6,5},{7,4},{8,11},{9,10},{10,... | collective-permute-start | bytes 1572872 | tf_op jit(solution)/shard_map/ppermute | solution.py:722
  261.0 23.4 %collective-permute-start.30 = (bf16[2,64,2048]{2,1,0:T(8,128)(2,1)}, bf16[2,64,2048]{2,1,0:T(8,128)(2,1)S(1)}, u32[]{:S(2)}, u32[]{:S(2)}) collective-permute-start(bf16[2,64,2048]{2,1,0:T(8,128)(2,1)} %copy-done.31), channel_id=1, source_target_pairs={{0,4},{4,0},{1,5},{5,1},{2,6},{6,2},{3,7},{7,3},{8,12},{12,8},{9,1... | collective-permute-start | bytes 1572872 | tf_op jit(solution)/shard_map/ppermute | solution.py:658
  262.5 22.7 %collective-permute-start.43 = (bf16[2,64,2048]{2,1,0:T(8,128)(2,1)}, bf16[2,64,2048]{2,1,0:T(8,128)(2,1)S(1)}, u32[]{:S(2)}, u32[]{:S(2)}) collective-permute-start(bf16[2,64,2048]{2,1,0:T(8,128)(2,1)} %get-tuple-element.174.refs_4_), channel_id=1, source_target_pairs={{0,4},{4,0},{1,5},{5,1},{2,6},{6,2},{3,7},{7,3},{8,12},{12,8},{9,1... | collective-permute-start | bytes 1572872 | tf_op jit(solution)/shard_map/ppermute | solution.py:658
  284.4 33.4 %collective-permute-start.29 = (bf16[2,64,2048]{2,1,0:T(8,128)(2,1)S(1)}, bf16[2,64,2048]{2,1,0:T(8,128)(2,1)S(1)}, u32[]{:S(2)}, u32[]{:S(2)}) collective-permute-start(bf16[2,64,2048]{2,1,0:T(8,128)(2,1)S(1)} %copy-done.30), channel_id=1, source_target_pairs={{0,4},{4,0},{1,5},{5,1},{2,6},{6,2},{3,7},{7,3},{8,12},{12,8},{9,1... | collective-permute-start | bytes 1572872 | tf_op jit(solution)/shard_map/ppermute | solution.py:658
  285.2 24.7 %collective-permute-start.42 = (bf16[2,64,2048]{2,1,0:T(8,128)(2,1)S(1)}, bf16[2,64,2048]{2,1,0:T(8,128)(2,1)S(1)}, u32[]{:S(2)}, u32[]{:S(2)}) collective-permute-start(bf16[2,64,2048]{2,1,0:T(8,128)(2,1)S(1)} %convert_add_fusion.3), channel_id=1, source_target_pairs={{0,1},{1,0},{2,3},{3,2},{4,5},{5,4},{6,7},{7,6},{8,9},{9,8},{10,11... | collective-permute-start | bytes 1572872 | tf_op jit(solution)/shard_map/ppermute | solution.py:722
  286.1 25.3 %collective-permute-start.40 = (bf16[2,64,2048]{2,1,0:T(8,128)(2,1)S(1)}, bf16[2,64,2048]{2,1,0:T(8,128)(2,1)S(1)}, u32[]{:S(2)}, u32[]{:S(2)}) collective-permute-start(bf16[2,64,2048]{2,1,0:T(8,128)(2,1)S(1)} %convert_add_fusion.4), channel_id=1, source_target_pairs={{0,2},{1,3},{2,0},{3,1},{4,6},{5,7},{6,4},{7,5},{8,10},{9,11},{10,... | collective-permute-start | bytes 1572872 | tf_op jit(solution)/shard_map/ppermute | solution.py:722
  287.6 23.8 %collective-permute-start.38 = (bf16[2,64,2048]{2,1,0:T(8,128)(2,1)S(1)}, bf16[2,64,2048]{2,1,0:T(8,128)(2,1)S(1)}, u32[]{:S(2)}, u32[]{:S(2)}) collective-permute-start(bf16[2,64,2048]{2,1,0:T(8,128)(2,1)S(1)} %convert_add_fusion.6), channel_id=1, source_target_pairs={{0,3},{1,2},{2,1},{3,0},{4,7},{5,6},{6,5},{7,4},{8,11},{9,10},{10,... | collective-permute-start | bytes 1572872 | tf_op jit(solution)/shard_map/ppermute | solution.py:722
  323.1 44.3 %all-to-all-start.4 = ((bf16[8,264,384]{2,1,0:T(8,128)(2,1)}), bf16[8,264,384]{2,1,0:T(8,128)(2,1)}, u32[]{:S(2)}, u32[]{:S(2)}) async-start(bf16[8,264,384]{2,1,0:T(8,128)(2,1)} %fusion.6), calls=%async_computation.4 | async-start | bytes 3244032 | tf_op jit(solution)/shard_map/all_to_all | solution.py:654
  369.8 47.8 %all-to-all-start.5 = ((bf16[8,448,256]{2,1,0:T(8,128)(2,1)}), bf16[8,448,256]{2,1,0:T(8,128)(2,1)}, u32[]{:S(2)}, u32[]{:S(2)}) async-start(bf16[8,448,256]{2,1,0:T(8,128)(2,1)} %pad_maximum_fusion), calls=%async_computation.5 | async-start | bytes 3670016 | tf_op jit(solution)/shard_map/all_to_all | solution.py:654
  (115 other events, 1208.6 us)

commit v2 on v1

--- a/solution.py
+++ b/solution.py
@@ -279,11 +279,7 @@
             pltpu.VMEM((heads, SKEW, 2 * seq_len), F32),
         ],
         compiler_params=pltpu.CompilerParams(vmem_limit_bytes=34 * 2**20),
-        cost_estimate=pl.CostEstimate(
-            flops=8 * seq_len * seq_len * width * 4,
-            bytes_accessed=2 * heads * seq_len * seq_len,
-            transcendentals=0,
-        ),
+        cost_estimate=pl.CostEstimate(flops=0, bytes_accessed=0, transcendentals=0),
         name="attention_backward",
     )(place, *other, *mine, prob, got, qkv)
 
@@ -408,6 +404,31 @@
     return outs[:count], outs[count], outs[-1] if table_shape is not None else None
 
 
+def rows_kernel(members, split, got_ref, first_ref, second_ref):
+    seqs = got_ref.shape[0] // members
+    rest = got_ref.shape[1] - split
+    for member in range(members):
+        total = sum(got_ref[seq * members + member].astype(F32) for seq in range(seqs))
+        first_ref[pl.ds(member * split, split), :] = total[:split]
+        second_ref[pl.ds(member * rest, rest), :] = total[split:]
+
+
+def owner_rows(got, members, split):
+    height, columns = got.shape[1:]
+    return pl.pallas_call(
+        functools.partial(rows_kernel, members, split),
+        out_shape=[
+            jax.ShapeDtypeStruct((members * split, columns), F32),
+            jax.ShapeDtypeStruct((members * (height - split), columns), F32),
+        ],
+        compiler_params=pltpu.CompilerParams(vmem_limit_bytes=32 * 2**20),
+        cost_estimate=pl.CostEstimate(
+            flops=0, bytes_accessed=4 * got.size, transcendentals=0
+        ),
+        name="owner_rows",
+    )(got)
+
+
 def rows_dot(left, right):
     return jnp.dot(left, right, preferred_element_type=F32)
 
@@ -490,7 +511,7 @@
         scratch_shapes=[pltpu.VMEM((rows, model), LOW)],
         compiler_params=pltpu.CompilerParams(vmem_limit_bytes=40 * 2**20),
         cost_estimate=pl.CostEstimate(
-            flops=2 * seq_len * depth * model, bytes_accessed=2 * seq_len * model, transcendentals=0
+            flops=0, bytes_accessed=0, transcendentals=0
         ),
         name=name,
     )(place, left, weight)
@@ -838,10 +859,6 @@
     def to_owners(grad):
         return exchange(grad, COLUMN)
 
-    def by_rows(got):
-        parts = got.reshape((seqs, members) + got.shape[1:]).astype(F32)
-        return jnp.sum(parts, axis=0).reshape(-1, shard)
-
     d_gate_up_w = contract_rows(hidden_two, after(d_both, *inner_cores)).astype(LOW)
     inner_two, inner_moved = sum_near_both(
         sum_mp(inner_cores, d_gate_up_w, *ffn_partial[0], *ffn_partial[1])
@@ -889,13 +906,15 @@
     )
     inner_sent, inner_kept = split_near(inner_pair)
     came = swap(
-        after(jnp.stack([ffn_sent, inner_sent]), d_qkv_got, ffn_gain, d_rows_sent), "near"
+        after(jnp.stack([ffn_sent, inner_sent]), here(pair_valid), d_rows_sent, ffn_gain), "near"
     )
     own_inputs = here(pair_inputs)
     inv_one = rms(own_inputs)
     grad_input = here(grad_one) + norm_grad(inner_kept + came[1].astype(F32), own_inputs * inv_one, inv_one)
     own_out = jnp.where(here(pair_valid), here(after_attn) + ffn_kept + came[0].astype(F32), 0.0)
-    owned = jnp.stack([own_out.astype(LOW), grad_input.astype(LOW)])
+    owned = after(
+        jnp.stack([own_out.astype(LOW), grad_input.astype(LOW)]), d_qkv_got
+    )
     rows_out = [jnp.zeros((mp_count, own_rows, model), LOW)] * 2
     blocks_out = [owned] + [shifted(owned, away) for away in range(1, mp_count)]
     d_rows = to_owners(after(d_rows_sent, d_qkv_got))
@@ -914,6 +933,7 @@
         (table_rows, heads_mp),
     )
     gains = jnp.concatenate([attn_gain, ffn_gain], 0)
+    d_w_down, d_w_out = owner_rows(d_rows, members, hidden_width)
     gains = sum((shifted(gains, away) for away in range(1, mp_count)), gains)
     return (
         layer_out,
@@ -922,12 +942,12 @@
         d_w_query,
         d_w_key,
         d_w_value,
-        by_rows(d_rows[:, hidden_width:]),
+        d_w_out,
         d_rel_table,
         gains[1],
         d_w_gate,
         d_w_up,
-        by_rows(d_rows[:, :hidden_width]),
+        d_w_down,
     )
 
 

time: 429 us -> 434 us (1.012)
    unnamed x144 -> x128, local copies, waits for them, and re-layouts: 15.3 us -> 7.47 us
    dynamic_update_slice x7 -> x8, local copies, waits for them, and re-layouts: 7.35 us -> 13 us  [in_order(): lax.dynamic_update_slice(rows, block[None, None], (at // 2, near_at ^ at...]
    ppermute x34, waiting for transfers between devices: 47 us -> 51.7 us  [swap(): return lax.ppermute(block, axis, [(0, 1), (1, 0)])]
  transfers between devices with their start and end apart: 67 -> 67, of which waited for: 35 -> 30; matrix products, arithmetic and copies ran while one was open for 17% -> 22% of each run, Pallas kernels for 12% -> 11%
where the time goes in v2:
time: 434 us; the launch traced here: 428 us
  waiting for transfers between devices  185 us (43%)
  starting transfers between devices  70.6 us (16%)
  Pallas kernels  70 us (16%)
  local copies, waits for them, and re-layouts  44.7 us (10%)
  other arithmetic  41.9 us (10%)
  matrix products  13.8 us (3%)
    ppermute x27, waiting for transfers between devices, shifted(): return lax.ppermute(block, 'mp', [(i, i ^ away) for i in range(mp_count)])  105 us
    ppermute x34, waiting for transfers between devices, swap(): return lax.ppermute(block, axis, [(0, 1), (1, 0)])  51.7 us
    ppermute x27, starting transfers between devices, shifted(): return lax.ppermute(block, 'mp', [(i, i ^ away) for i in range(mp_count)])  32.1 us
    all_to_all x6, starting transfers between devices, exchange(): return lax.all_to_all(blocks, axes, split_axis=0, concat_axis=0, tiled=True)  28.6 us
    all_to_all x6, waiting for transfers between devices, exchange(): return lax.all_to_all(blocks, axes, split_axis=0, concat_axis=0, tiled=True)  28.6 us
    pallas_call x1, Pallas kernels, feed_forward(): pl.pallas_call(functools.partial(ffn_kernel, near_count, count), grid=(CO...  19.8 us
    pallas_call x1, Pallas kernels, attention_backward(): pl.pallas_call(functools.partial(backward_kernel, heads, shard, near_coun...  14.5 us
    dot_general x3, matrix products, contract_rows(): lax.dot_general(left, right, (((0,), (0,)), ((), ())), preferred_element_...  13.8 us
  transfers between devices with their start and end apart: 67, of which 30 were waited for; matrix products, arithmetic and copies ran while one was open for 22% of the time, Pallas kernels for 11%

profile of v2, /device:TPU:0, one launch (start us, length us, event | category | flops | bytes accessed | tf_op | source)
XLA Modules:
  0.0 427.7 jit_solution(13579911773329723193)
XLA Ops:
  15.3 6.2 %collective-permute-done = bf16[2,64,2048]{2,1,0:T(8,128)(2,1)} collective-permute-done((bf16[2,64,2048]{2,1,0:T(8,128)(2,1)}, bf16[2,64,2048]{2,1,0:T(8,128)(2,1)}, u32[]{:S(2)}, u32[]{:S(2)}) %collective-permute-start) | collective-permute-done | bytes 524320 | tf_op jit(solution)/shard_map/ppermute | solution.py:679
  38.6 8.9 %collective-permute-done.2 = bf16[2,64,2048]{2,1,0:T(8,128)(2,1)} collective-permute-done((bf16[2,64,2048]{2,1,0:T(8,128)(2,1)}, bf16[2,64,2048]{2,1,0:T(8,128)(2,1)}, u32[]{:S(2)}, u32[]{:S(2)}) %collective-permute-start.2) | collective-permute-done | bytes 524320 | tf_op jit(solution)/shard_map/ppermute | solution.py:743
  74.3 7.1 %all-to-all-start.1 = ((bf16[8,576,256]{2,1,0:T(8,128)(2,1)}), bf16[8,576,256]{2,1,0:T(8,128)(2,1)}, u32[]{:S(2)}, u32[]{:S(2)}) async-start(bf16[8,576,256]{2,1,0:T(8,128)(2,1)} %copy-done.11), calls=%async_computation.1 | async-start | bytes 4718592 | tf_op jit(solution)/shard_map/all_to_all | solution.py:675
  85.2 10.7 %attention_forward.1 = (bf16[1024,384]{1,0:T(8,128)(2,1)S(1)}, bf16[1024,128]{1,0:T(8,128)(2,1)S(1)}, bf16[2,1024,1024]{2,1,0:T(8,128)(2,1)S(1)}, bf16[2,64,2048...) custom-call(s32[5]{0:T(128)S(1)} %stack.62.place_ref, ...), custom_call_target="tpu_custom_call" | custom-call | tf_op jit(solution)/shard_map/attention_forward/pallas_call | solution.py:146
  108.7 8.3 %collective-permute-done.11 = bf16[2,64,2048]{2,1,0:T(8,128)(2,1)S(1)} collective-permute-done((bf16[2,64,2048]{2,1,0:T(8,128)(2,1)S(1)}, bf16[2,64,2048]{2,1,0:T(8,128)(2,1)S(1)}, u32[]{:S(2)}, u32[]{:S(2)}) %collective-permute-start.11) | collective-permute-done | bytes 524320 | tf_op jit(solution)/shard_map/ppermute | solution.py:743
  117.0 10.8 %collective-permute-done.13 = bf16[2,64,2048]{2,1,0:T(8,128)(2,1)S(1)} collective-permute-done((bf16[2,64,2048]{2,1,0:T(8,128)(2,1)S(1)}, bf16[2,64,2048]{2,1,0:T(8,128)(2,1)S(1)}, u32[]{:S(2)}, u32[]{:S(2)}) %collective-permute-start.13) | collective-permute-done | bytes 524320 | tf_op jit(solution)/shard_map/ppermute | solution.py:743
  128.3 7.9 %all-to-all-done.1.refs_9_.weight_ref = bf16[8,576,256]{2,1,0:T(8,128)(2,1)} async-done(((bf16[8,576,256]{2,1,0:T(8,128)(2,1)}), bf16[8,576,256]{2,1,0:T(8,128)(2,1)}, u32[]{:S(2)}, u32[]{:S(2)}) %all-to-all-start.1) | async-done | bytes 2359328 | tf_op jit(solution)/shard_map/all_to_all | solution.py:675
  136.2 13.5 %collective-permute-done.17 = bf16[2,64,2048]{2,1,0:T(8,128)(2,1)S(1)} collective-permute-done((bf16[2,64,2048]{2,1,0:T(8,128)(2,1)S(1)}, bf16[2,64,2048]{2,1,0:T(8,128)(2,1)S(1)}, u32[]{:S(2)}, u32[]{:S(2)}) %collective-permute-start.17) | collective-permute-done | bytes 524320 | tf_op jit(solution)/shard_map/ppermute | solution.py:679
  160.8 11.2 %collective-permute-done.19.refs_5_ = bf16[2,64,2048]{2,1,0:T(8,128)(2,1)S(1)} collective-permute-done((bf16[2,64,2048]{2,1,0:T(8,128)(2,1)S(1)}, bf16[2,64,2048]{2,1,0:T(8,128)(2,1)S(1)}, u32[]{:S(2)}, u32[]{:S(2)}) %collective-permute-start.19) | collective-permute-done | bytes 524320 | tf_op jit(solution)/shard_map/ppermute | solution.py:743
  172.0 10.1 %collective-permute-done.21.refs_6_ = bf16[2,64,2048]{2,1,0:T(8,128)(2,1)S(1)} collective-permute-done((bf16[2,64,2048]{2,1,0:T(8,128)(2,1)S(1)}, bf16[2,64,2048]{2,1,0:T(8,128)(2,1)S(1)}, u32[]{:S(2)}, u32[]{:S(2)}) %collective-permute-start.21) | collective-permute-done | bytes 524320 | tf_op jit(solution)/shard_map/ppermute | solution.py:743
  185.8 6.2 %all-to-all-done.2.refs_10_ = bf16[8,256,384]{2,1,0:T(8,128)(2,1)} async-done(((bf16[8,256,384]{2,1,0:T(8,128)(2,1)}), bf16[8,256,384]{2,1,0:T(8,128)(2,1)}, u32[]{:S(2)}, u32[]{:S(2)}) %all-to-all-start.2) | async-done | bytes 1572896 | tf_op jit(solution)/shard_map/all_to_all | solution.py:675
  192.0 19.8 %feed_forward.1 = (bf16[2,64,2048]{2,1,0:T(8,128)(2,1)}, bf16[2,64,2048]{2,1,0:T(8,128)(2,1)}, bf16[2,64,2048]{2,1,0:T(8,128)(2,1)}, bf16[2,64,2048]{2,1,0:T(8,1...) custom-call(s32[5]{0:T(128)} %copy-done.27, ...), custom_call_target="tpu_custom_call" | custom-call | flops 8053063680 | bytes 25165824 | tf_op jit(solution)/shard_map/feed_forward/pallas_call | solution.py:637
  220.6 5.7 %ffn_out.1 = (bf16[2,64,2048]{2,1,0:T(8,128)(2,1)S(1)}, bf16[2,64,2048]{2,1,0:T(8,128)(2,1)S(1)}, bf16[2,64,2048]{2,1,0:T(8,128)(2,1)}, bf16[2,64,2048]{2,1,0:T(...) custom-call(s32[5]{0:T(128)S(1)} %copy-done.28, ...), custom_call_target="tpu_custom_call" | custom-call | tf_op jit(solution)/shard_map/ffn_out/pallas_call | solution.py:501
  231.3 10.4 %collective-permute-done.32 = bf16[2,64,2048]{2,1,0:T(8,128)(2,1)S(1)} collective-permute-done((bf16[2,64,2048]{2,1,0:T(8,128)(2,1)S(1)}, bf16[2,64,2048]{2,1,0:T(8,128)(2,1)S(1)}, u32[]{:S(2)}, u32[]{:S(2)}) %collective-permute-start.32) | collective-permute-done | bytes 524320 | tf_op jit(solution)/shard_map/ppermute | solution.py:743
  244.7 11.3 %collective-permute-done.34 = bf16[2,64,2048]{2,1,0:T(8,128)(2,1)S(1)} collective-permute-done((bf16[2,64,2048]{2,1,0:T(8,128)(2,1)S(1)}, bf16[2,64,2048]{2,1,0:T(8,128)(2,1)S(1)}, u32[]{:S(2)}, u32[]{:S(2)}) %collective-permute-start.34) | collective-permute-done | bytes 524320 | tf_op jit(solution)/shard_map/ppermute | solution.py:679
  273.9 8.6 %collective-permute-done.36.refs_6_ = bf16[2,64,2048]{2,1,0:T(8,128)(2,1)} collective-permute-done((bf16[2,64,2048]{2,1,0:T(8,128)(2,1)S(1)}, bf16[2,64,2048]{2,1,0:T(8,128)(2,1)}, u32[]{:S(2)}, u32[]{:S(2)}) %collective-permute-start.36) | collective-permute-done | bytes 524320 | tf_op jit(solution)/shard_map/ppermute | solution.py:743
  290.9 14.5 %attention_backward.1 = (bf16[1024,384]{1,0:T(8,128)(2,1)S(1)}, f32[32,128]{1,0:T(8,128)S(1)}, bf16[1024,2048]{1,0:T(8,128)(2,1)S(1)}) custom-call(s32[5]{0:T(128)S(1)} %copy-done.28, bf16[2,64,2048]{2,1,0:T(8,128)(2,1)S(1)} %collective-permute-done.43.refs_0_, bf16[2,64,2048]{2,1,0:T(8,128)(2,1)S(1)} %collective-permute-done.44.refs_1_, ...), custom_call_target="tpu_custom_call" | custom-call | tf_op jit(solution)/shard_map/attention_backward/pallas_call | solution.py:256
  305.4 6.1 %convolution_convert_fusion.1 = bf16[2048,384]{1,0:T(8,128)(2,1)S(1)} fusion(bf16[1024,2048]{1,0:T(8,128)(2,1)} %bitcast.32, bf16[1024,384]{1,0:T(8,128)(2,1)S(1)} %get-tuple-element.146.left_ref), kind=kOutput, calls=%fused_computation.3 | convolution fusion | flops 1611399168 | bytes 6553600 | tf_op jit(solution)/shard_map/dot_general | solution.py:441
  339.8 7.6 %collective-permute-done.51 = bf16[2,64,2048]{2,1,0:T(8,128)(2,1)} collective-permute-done((bf16[2,64,2048]{2,1,0:T(8,128)(2,1)}, bf16[2,64,2048]{2,1,0:T(8,128)(2,1)}, u32[]{:S(2)}, u32[]{:S(2)}) %collective-permute-start.51) | collective-permute-done | bytes 524320 | tf_op jit(solution)/shard_map/ppermute | solution.py:743
  349.5 6.3 %owner_grads.2 = (f32[256,1280]{1,0:T(8,128)}, f32[256,1280]{1,0:T(8,128)}, f32[1,256]{1,0:T(1,128)S(1)}) custom-call(bf16[8,256,640]{2,1,0:T(8,128)(2,1)} %all-to-all-done.3.refs_0_.refs_1_, bf16[8,256,640]{2,1,0:T(8,128)(2,1)} %all-to-all-done.3.refs_0_.refs_1_, f32[256,1280]{1,0:T(8,128)S(1)} %copy-done.5, f32[256,1280]{1,0:T(8,128)S(1)} %copy-done.7, ...), custom_call_target="tpu_custom_call" | custom-call | bytes 6553600 | tf_op jit(solution)/shard_map/owner_grads/pallas_call | solution.py:387
  358.0 17.9 %collective-permute-done.54 = bf16[2,64,2048]{2,1,0:T(8,128)(2,1)S(1)} collective-permute-done((bf16[2,64,2048]{2,1,0:T(8,128)(2,1)S(1)}, bf16[2,64,2048]{2,1,0:T(8,128)(2,1)S(1)}, u32[]{:S(2)}, u32[]{:S(2)}) %collective-permute-start.54) | collective-permute-done | bytes 524320 | tf_op jit(solution)/shard_map/ppermute | solution.py:679
  387.4 11.0 %collective-permute-done.55 = bf16[2,64,2048]{2,1,0:T(8,128)(2,1)S(1)} collective-permute-done((bf16[2,64,2048]{2,1,0:T(8,128)(2,1)S(1)}, bf16[2,64,2048]{2,1,0:T(8,128)(2,1)S(1)}, u32[]{:S(2)}, u32[]{:S(2)}) %collective-permute-start.55) | collective-permute-done | bytes 524320 | tf_op jit(solution)/shard_map/ppermute | solution.py:743
  404.4 5.8 %collective-permute-done.56 = bf16[2,64,2048]{2,1,0:T(8,128)(2,1)S(1)} collective-permute-done((bf16[2,64,2048]{2,1,0:T(8,128)(2,1)S(1)}, bf16[2,64,2048]{2,1,0:T(8,128)(2,1)S(1)}, u32[]{:S(2)}, u32[]{:S(2)}) %collective-permute-start.56) | collective-permute-done | bytes 524320 | tf_op jit(solution)/shard_map/ppermute | solution.py:743
  411.8 12.8 %all-to-all-done.5.got_ref = bf16[8,448,256]{2,1,0:T(8,128)(2,1)} async-done(((bf16[8,448,256]{2,1,0:T(8,128)(2,1)}), bf16[8,448,256]{2,1,0:T(8,128)(2,1)}, u32[]{:S(2)}, u32[]{:S(2)}) %all-to-all-start.5) | async-done | bytes 1835040 | tf_op jit(solution)/shard_map/all_to_all | solution.py:675
  (345 shorter events, 187.2 us)
Async XLA Ops:
  0.6 51.9 %collective-permute-start.4 = (bf16[256,2048]{1,0:T(8,128)(2,1)}, bf16[256,2048]{1,0:T(8,128)(2,1)}, u32[]{:S(2)}, u32[]{:S(2)}) collective-permute-start(bf16[256,2048]{1,0:T(8,128)(2,1)} %param.13), channel_id=1, source_target_pairs={{0,4},{4,0},{1,5},{5,1},{2,6},{6,2},{3,7},{7,3},{8,12},{12,8},{9,1... | collective-permute-start | bytes 3145736 | tf_op jit(solution)/shard_map/ppermute | solution.py:679
  9.8 64.5 %all-to-all-start = ((bf16[8,264,512]{2,1,0:T(8,128)(2,1)}), bf16[8,264,512]{2,1,0:T(8,128)(2,1)S(1)}, u32[]{:S(2)}, u32[]{:S(2)}) async-start(bf16[8,264,512]{2,1,0:T(8,128)(2,1)} %attention_blocks.1), calls=%async_computation | async-start | bytes 4325376 | tf_op jit(solution)/shard_map/all_to_all | solution.py:675
  23.5 24.0 %collective-permute-start.2 = (bf16[2,64,2048]{2,1,0:T(8,128)(2,1)}, bf16[2,64,2048]{2,1,0:T(8,128)(2,1)}, u32[]{:S(2)}, u32[]{:S(2)}) collective-permute-start(bf16[2,64,2048]{2,1,0:T(8,128)(2,1)} %collective-permute-done), channel_id=1, source_target_pairs={{0,2},{1,3},{2,0},{3,1},{4,6},{5,7},{6,4},{7,5},{8,10},{9,11},{10,... | collective-permute-start | bytes 1572872 | tf_op jit(solution)/shard_map/ppermute | solution.py:743
  31.3 26.1 %collective-permute-start.5 = (bf16[2,64,2048]{2,1,0:T(8,128)(2,1)}, bf16[2,64,2048]{2,1,0:T(8,128)(2,1)S(1)}, u32[]{:S(2)}, u32[]{:S(2)}) collective-permute-start(bf16[2,64,2048]{2,1,0:T(8,128)(2,1)} %collective-permute-done), channel_id=1, source_target_pairs={{0,4},{4,0},{1,5},{5,1},{2,6},{6,2},{3,7},{7,3},{8,12},{12,8},{9,1... | collective-permute-start | bytes 1572872 | tf_op jit(solution)/shard_map/ppermute | solution.py:679
  54.4 50.8 %collective-permute-start.16 = (bf16[256,2048]{1,0:T(8,128)(2,1)}, bf16[256,2048]{1,0:T(8,128)(2,1)}, u32[]{:S(2)}, u32[]{:S(2)}) collective-permute-start(bf16[256,2048]{1,0:T(8,128)(2,1)} %param.14), channel_id=1, source_target_pairs={{0,4},{4,0},{1,5},{5,1},{2,6},{6,2},{3,7},{7,3},{8,12},{12,8},{9,1... | collective-permute-start | bytes 3145736 | tf_op jit(solution)/shard_map/ppermute | solution.py:679
  74.3 61.9 %all-to-all-start.1 = ((bf16[8,576,256]{2,1,0:T(8,128)(2,1)}), bf16[8,576,256]{2,1,0:T(8,128)(2,1)}, u32[]{:S(2)}, u32[]{:S(2)}) async-start(bf16[8,576,256]{2,1,0:T(8,128)(2,1)} %copy-done.11), calls=%async_computation.1 | async-start | bytes 4718592 | tf_op jit(solution)/shard_map/all_to_all | solution.py:675
  102.9 24.8 %collective-permute-start.13 = (bf16[2,64,2048]{2,1,0:T(8,128)(2,1)S(1)}, bf16[2,64,2048]{2,1,0:T(8,128)(2,1)S(1)}, u32[]{:S(2)}, u32[]{:S(2)}) collective-permute-start(bf16[2,64,2048]{2,1,0:T(8,128)(2,1)S(1)} %add_convert_fusion.5), channel_id=1, source_target_pairs={{0,2},{1,3},{2,0},{3,1},{4,6},{5,7},{6,4},{7,5},{8,10},{9,11},{10,... | collective-permute-start | bytes 1572872 | tf_op jit(solution)/shard_map/ppermute | solution.py:743
  104.4 23.5 %collective-permute-start.15 = (bf16[2,64,2048]{2,1,0:T(8,128)(2,1)S(1)}, bf16[2,64,2048]{2,1,0:T(8,128)(2,1)S(1)}, u32[]{:S(2)}, u32[]{:S(2)}) collective-permute-start(bf16[2,64,2048]{2,1,0:T(8,128)(2,1)S(1)} %add_convert_fusion.4), channel_id=1, source_target_pairs={{0,1},{1,0},{2,3},{3,2},{4,5},{5,4},{6,7},{7,6},{8,9},{9,8},{10,11... | collective-permute-start | bytes 1572872 | tf_op jit(solution)/shard_map/ppermute | solution.py:743
  149.7 42.3 %all-to-all-start.2 = ((bf16[8,256,384]{2,1,0:T(8,128)(2,1)}), bf16[8,256,384]{2,1,0:T(8,128)(2,1)}, u32[]{:S(2)}, u32[]{:S(2)}) async-start(bf16[8,256,384]{2,1,0:T(8,128)(2,1)} %copy-done.15), calls=%async_computation.2 | async-start | bytes 3145728 | tf_op jit(solution)/shard_map/all_to_all | solution.py:675
  158.5 23.6 %collective-permute-start.21 = (bf16[2,64,2048]{2,1,0:T(8,128)(2,1)S(1)}, bf16[2,64,2048]{2,1,0:T(8,128)(2,1)S(1)}, u32[]{:S(2)}, u32[]{:S(2)}) collective-permute-start(bf16[2,64,2048]{2,1,0:T(8,128)(2,1)S(1)} %multiply_convert_fusion.1.refs_4_), channel_id=1, source_target_pairs={{0,2},{1,3},{2,0},{3,1},{4,6},{5,7},{6,4},{7,5},{8,10},{9,11},{10,... | collective-permute-start | bytes 1572872 | tf_op jit(solution)/shard_map/ppermute | solution.py:743
  159.3 24.4 %collective-permute-start.23 = (bf16[2,64,2048]{2,1,0:T(8,128)(2,1)S(1)}, bf16[2,64,2048]{2,1,0:T(8,128)(2,1)S(1)}, u32[]{:S(2)}, u32[]{:S(2)}) collective-permute-start(bf16[2,64,2048]{2,1,0:T(8,128)(2,1)S(1)} %multiply_convert_fusion.1.refs_4_), channel_id=1, source_target_pairs={{0,3},{1,2},{2,1},{3,0},{4,7},{5,6},{6,5},{7,4},{8,11},{9,10},{10,... | collective-permute-start | bytes 1572872 | tf_op jit(solution)/shard_map/ppermute | solution.py:743
  218.4 23.3 %collective-permute-start.32 = (bf16[2,64,2048]{2,1,0:T(8,128)(2,1)S(1)}, bf16[2,64,2048]{2,1,0:T(8,128)(2,1)S(1)}, u32[]{:S(2)}, u32[]{:S(2)}) collective-permute-start(bf16[2,64,2048]{2,1,0:T(8,128)(2,1)S(1)} %fusion.11), channel_id=1, source_target_pairs={{0,2},{1,3},{2,0},{3,1},{4,6},{5,7},{6,4},{7,5},{8,10},{9,11},{10,... | collective-permute-start | bytes 1572872 | tf_op jit(solution)/shard_map/ppermute | solution.py:743
  244.1 23.6 %collective-permute-start.30 = (bf16[2,64,2048]{2,1,0:T(8,128)(2,1)}, bf16[2,64,2048]{2,1,0:T(8,128)(2,1)}, u32[]{:S(2)}, u32[]{:S(2)}) collective-permute-start(bf16[2,64,2048]{2,1,0:T(8,128)(2,1)} %get-tuple-element.128), channel_id=1, source_target_pairs={{0,4},{4,0},{1,5},{5,1},{2,6},{6,2},{3,7},{7,3},{8,12},{12,8},{9,1... | collective-permute-start | bytes 1572872 | tf_op jit(solution)/shard_map/ppermute | solution.py:679
  244.2 25.7 %collective-permute-start.39 = (bf16[2,64,2048]{2,1,0:T(8,128)(2,1)}, bf16[2,64,2048]{2,1,0:T(8,128)(2,1)}, u32[]{:S(2)}, u32[]{:S(2)}) collective-permute-start(bf16[2,64,2048]{2,1,0:T(8,128)(2,1)} %get-tuple-element.135), channel_id=1, source_target_pairs={{0,4},{4,0},{1,5},{5,1},{2,6},{6,2},{3,7},{7,3},{8,12},{12,8},{9,1... | collective-permute-start | bytes 1572872 | tf_op jit(solution)/shard_map/ppermute | solution.py:679
  263.0 65.0 %all-to-all-start.3 = ((bf16[8,256,640]{2,1,0:T(8,128)(2,1)}), bf16[8,256,640]{2,1,0:T(8,128)(2,1)}, u32[]{:S(2)}, u32[]{:S(2)}) async-start(bf16[8,256,640]{2,1,0:T(8,128)(2,1)} %bitcast.100), calls=%async_computation.3 | async-start | bytes 5242880 | tf_op jit(solution)/shard_map/all_to_all | solution.py:675
  285.6 32.8 %collective-permute-start.29 = (bf16[2,64,2048]{2,1,0:T(8,128)(2,1)}, bf16[2,64,2048]{2,1,0:T(8,128)(2,1)S(1)}, u32[]{:S(2)}, u32[]{:S(2)}) collective-permute-start(bf16[2,64,2048]{2,1,0:T(8,128)(2,1)} %copy-done.31), channel_id=1, source_target_pairs={{0,4},{4,0},{1,5},{5,1},{2,6},{6,2},{3,7},{7,3},{8,12},{12,8},{9,1... | collective-permute-start | bytes 1572872 | tf_op jit(solution)/shard_map/ppermute | solution.py:679
  287.3 25.6 %collective-permute-start.38 = (bf16[2,64,2048]{2,1,0:T(8,128)(2,1)S(1)}, bf16[2,64,2048]{2,1,0:T(8,128)(2,1)S(1)}, u32[]{:S(2)}, u32[]{:S(2)}) collective-permute-start(bf16[2,64,2048]{2,1,0:T(8,128)(2,1)S(1)} %convert_add_fusion.6), channel_id=1, source_target_pairs={{0,3},{1,2},{2,1},{3,0},{4,7},{5,6},{6,5},{7,4},{8,11},{9,10},{10,... | collective-permute-start | bytes 1572872 | tf_op jit(solution)/shard_map/ppermute | solution.py:743
  289.2 24.2 %collective-permute-start.40 = (bf16[2,64,2048]{2,1,0:T(8,128)(2,1)S(1)}, bf16[2,64,2048]{2,1,0:T(8,128)(2,1)S(1)}, u32[]{:S(2)}, u32[]{:S(2)}) collective-permute-start(bf16[2,64,2048]{2,1,0:T(8,128)(2,1)S(1)} %convert_add_fusion.4), channel_id=1, source_target_pairs={{0,2},{1,3},{2,0},{3,1},{4,6},{5,7},{6,4},{7,5},{8,10},{9,11},{10,... | collective-permute-start | bytes 1572872 | tf_op jit(solution)/shard_map/ppermute | solution.py:743
  289.6 23.8 %collective-permute-start.42 = (bf16[2,64,2048]{2,1,0:T(8,128)(2,1)S(1)}, bf16[2,64,2048]{2,1,0:T(8,128)(2,1)S(1)}, u32[]{:S(2)}, u32[]{:S(2)}) collective-permute-start(bf16[2,64,2048]{2,1,0:T(8,128)(2,1)S(1)} %convert_add_fusion.3), channel_id=1, source_target_pairs={{0,1},{1,0},{2,3},{3,2},{4,5},{5,4},{6,7},{7,6},{8,9},{9,8},{10,11... | collective-permute-start | bytes 1572872 | tf_op jit(solution)/shard_map/ppermute | solution.py:743
  323.6 23.7 %collective-permute-start.51 = (bf16[2,64,2048]{2,1,0:T(8,128)(2,1)}, bf16[2,64,2048]{2,1,0:T(8,128)(2,1)}, u32[]{:S(2)}, u32[]{:S(2)}) collective-permute-start(bf16[2,64,2048]{2,1,0:T(8,128)(2,1)} %add_convert_fusion.1), channel_id=1, source_target_pairs={{0,2},{1,3},{2,0},{3,1},{4,6},{5,7},{6,4},{7,5},{8,10},{9,11},{10,... | collective-permute-start | bytes 1572872 | tf_op jit(solution)/shard_map/ppermute | solution.py:743
  328.1 48.6 %all-to-all-start.4 = ((bf16[8,264,384]{2,1,0:T(8,128)(2,1)}), bf16[8,264,384]{2,1,0:T(8,128)(2,1)S(1)}, u32[]{:S(2)}, u32[]{:S(2)}) async-start(bf16[8,264,384]{2,1,0:T(8,128)(2,1)} %fusion.6), calls=%async_computation.4 | async-start | bytes 3244032 | tf_op jit(solution)/shard_map/all_to_all | solution.py:675
  376.7 47.9 %all-to-all-start.5 = ((bf16[8,448,256]{2,1,0:T(8,128)(2,1)}), bf16[8,448,256]{2,1,0:T(8,128)(2,1)}, u32[]{:S(2)}, u32[]{:S(2)}) async-start(bf16[8,448,256]{2,1,0:T(8,128)(2,1)} %pad_maximum_fusion), calls=%async_computation.5 | async-start | bytes 3670016 | tf_op jit(solution)/shard_map/all_to_all | solution.py:675
  385.0 25.2 %collective-permute-start.56 = (bf16[2,64,2048]{2,1,0:T(8,128)(2,1)S(1)}, bf16[2,64,2048]{2,1,0:T(8,128)(2,1)S(1)}, u32[]{:S(2)}, u32[]{:S(2)}) collective-permute-start(bf16[2,64,2048]{2,1,0:T(8,128)(2,1)S(1)} %pad_maximum_fusion.3), channel_id=1, source_target_pairs={{0,2},{1,3},{2,0},{3,1},{4,6},{5,7},{6,4},{7,5},{8,10},{9,11},{10,... | collective-permute-start | bytes 1572872 | tf_op jit(solution)/shard_map/ppermute | solution.py:743
  385.9 24.3 %collective-permute-start.57 = (bf16[2,64,2048]{2,1,0:T(8,128)(2,1)S(1)}, bf16[2,64,2048]{2,1,0:T(8,128)(2,1)S(1)}, u32[]{:S(2)}, u32[]{:S(2)}) collective-permute-start(bf16[2,64,2048]{2,1,0:T(8,128)(2,1)S(1)} %pad_maximum_fusion.3), channel_id=1, source_target_pairs={{0,3},{1,2},{2,1},{3,0},{4,7},{5,6},{6,5},{7,4},{8,11},{9,10},{10,... | collective-permute-start | bytes 1572872 | tf_op jit(solution)/shard_map/ppermute | solution.py:743
  (107 other events, 1136.3 us)

commit v3 on v2

--- a/solution.py
+++ b/solution.py
@@ -462,6 +462,37 @@
         write(mine_refs)
 
 
+def place_kernel(near_count, place_ref, *refs):
+    parts, outs, copied = refs[:-3], refs[-3:-1], refs[-1]
+    each = len(parts) // 2
+    rows = parts[0].shape[0]
+    copies = []
+    for i, ref in enumerate(parts):
+        at = i % each
+        first = (at // 2) * near_count + lax.bitwise_xor(place_ref[4], at % 2)
+        place = outs[i // each].at[pl.ds(pl.multiple_of(first * rows, rows), rows), :]
+        copies.append(pltpu.make_async_copy(ref, place, copied.at[i]))
+    for copy in copies:
+        copy.start()
+    for copy in copies:
+        copy.wait()
+
+
+def place_rows(first, second, place, near_count):
+    rows, model = first[0].shape
+    shape = jax.ShapeDtypeStruct((rows * len(first), model), LOW)
+    somewhere = pl.BlockSpec(memory_space=pl.ANY)
+    return pl.pallas_call(
+        functools.partial(place_kernel, near_count),
+        in_specs=[pl.BlockSpec(memory_space=pltpu.SMEM)] + [somewhere] * (2 * len(first)),
+        out_specs=[somewhere] * 2,
+        out_shape=[shape] * 2,
+        scratch_shapes=[pltpu.SemaphoreType.DMA((2 * len(first),))],
+        cost_estimate=pl.CostEstimate(flops=0, bytes_accessed=0, transcendentals=0),
+        name="place_rows",
+    )(place, *first, *second)
+
+
 def take_rows(step, near_count, mp_at, other_refs, mine_refs, rows_ref):
     own_rows = other_refs[0].shape[1]
 
@@ -761,14 +792,6 @@
             halves.append([rows[i].reshape(tok_rows, model) for i in range(len(blocks))])
         return *halves, made
 
-    def in_order(own, moved, core, core_moved):
-        rows = jnp.zeros((CORES, near_count, tok_rows, model), own.dtype)
-        for at, block in enumerate((own, moved, core, core_moved)):
-            rows = lax.dynamic_update_slice(
-                rows, block[None, None], (at // 2, near_at ^ (at % 2), 0, 0)
-            )
-        return rows.reshape(seq_len, model)
-
     def gather_rows(near):
         mine = [near] + [shifted(near, away) for away in range(1, mp_count)]
         return mine, [swap(block, "core") for block in mine]
@@ -837,9 +860,9 @@
     qkv, attended, prob, out_mine, out_other = attention_forward(
         parts, attn_got, table, place, heads, shard, mp_count
     )
-    normed_rows, grad_two = in_order(*parts), in_order(*grad_parts)
+    normed_rows, grad_two = place_rows(parts, grad_parts, after(place, attended), near_count)
     mixed, mixed_moved = sum_near_both(
-        after(sum_mp(sum_cores(out_mine, out_other)), first_got, grad_two, normed_rows)
+        after(sum_mp(sum_cores(out_mine, out_other), grad_two, normed_rows), first_got)
     )
     second_got = exchange(after(ffn_second, mixed_moved), COLUMN)
 

time: 434 us -> 655 us (1.51)
  Pallas kernels: 70 us -> 326 us
  waiting for transfers between devices: 185 us -> 164 us
  local copies, waits for them, and re-layouts: 44.7 us -> 27.4 us
    pallas_call x0 -> x1, Pallas kernels: none -> 256 us  [place_rows(): pl.pallas_call(functools.partial(place_kernel, near_count), in_specs=[pl....]
    ppermute x27, waiting for transfers between devices: 105 us -> 89.8 us  [shifted(): return lax.ppermute(block, 'mp', [(i, i ^ away) for i in range(mp_count)])]
    dynamic_update_slice x8 -> x0, local copies, waits for them, and re-layouts: 13 us -> none  [in_order(): lax.dynamic_update_slice(rows, block[None, None], (at // 2, near_at ^ at...]
  transfers between devices with their start and end apart: 67 -> 67, of which waited for: 30 -> 26; matrix products, arithmetic and copies ran while one was open for 22% -> 11% of each run, Pallas kernels for 11% -> 47%
where the time goes in v3:
time: 655 us; the launch traced here: 645 us
  Pallas kernels  326 us (50%)
  waiting for transfers between devices  164 us (25%)
  starting transfers between devices  69.5 us (11%)
  other arithmetic  46.5 us (7%)
  local copies, waits for them, and re-layouts  27.4 us (4%)
  matrix products  10.2 us (2%)
    pallas_call x1, Pallas kernels, place_rows(): pl.pallas_call(functools.partial(place_kernel, near_count), in_specs=[pl....  256 us
    ppermute x27, waiting for transfers between devices, shifted(): return lax.ppermute(block, 'mp', [(i, i ^ away) for i in range(mp_count)])  89.8 us
    ppermute x34, waiting for transfers between devices, swap(): return lax.ppermute(block, axis, [(0, 1), (1, 0)])  51.8 us
    ppermute x27, starting transfers between devices, shifted(): return lax.ppermute(block, 'mp', [(i, i ^ away) for i in range(mp_count)])  32.2 us
    all_to_all x6, starting transfers between devices, exchange(): return lax.all_to_all(blocks, axes, split_axis=0, concat_axis=0, tiled=True)  25.6 us
    all_to_all x6, waiting for transfers between devices, exchange(): return lax.all_to_all(blocks, axes, split_axis=0, concat_axis=0, tiled=True)  22.2 us
    pallas_call x1, Pallas kernels, feed_forward(): pl.pallas_call(functools.partial(ffn_kernel, near_count, count), grid=(CO...  19.8 us
    pallas_call x1, Pallas kernels, attention_backward(): pl.pallas_call(functools.partial(backward_kernel, heads, shard, near_coun...  14.7 us
  transfers between devices with their start and end apart: 67, of which 26 were waited for; matrix products, arithmetic and copies ran while one was open for 11% of the time, Pallas kernels for 47%

profile of v3, /device:TPU:0, one launch (start us, length us, event | category | flops | bytes accessed | tf_op | source)
XLA Modules:
  0.0 645.3 jit_solution(7721298465790713486)
XLA Ops:
  14.5 5.4 collective-permute-done
  28.8 6.4 collective-permute-done.1
  37.1 6.4 collective-permute-done.2
  72.9 11.6 %attention_forward.1 = (bf16[1024,384]{1,0:T(8,128)(2,1)S(1)}, bf16[1024,128]{1,0:T(8,128)(2,1)S(1)}, bf16[2,1024,1024]{2,1,0:T(8,128)(2,1)S(1)}, bf16[2,64,2048...) custom-call(s32[5]{0:T(128)S(1)} %stack.62.place_ref, ...), custom_call_target="tpu_custom_call" | custom-call | tf_op jit(solution)/shard_map/attention_forward/pallas_call | solution.py:146
  95.3 256.1 %place_rows.1 = (bf16[1024,2048]{1,0:T(8,128)(2,1)}, bf16[1024,2048]{1,0:T(8,128)(2,1)}) custom-call(s32[5]{0:T(128)} %copy-done.29, bf16[256,2048]{1,0:T(8,128)(2,1)} %fusion.2.refs_0_, bf16[256,2048]{1,0:T(8,128)(2,1)} %copy-done.1, bf16[256,2048]{1,0:T(8,128)(2,1)} %fusion.4.refs_2_, bf16[256,2048]{1,0:T(8,128)(2,1)} %copy-done, ...), custom_call_target="tpu_custom_call" | custom-call | tf_op jit(solution)/shard_map/place_rows/pallas_call | solution.py:485
  355.4 12.6 %collective-permute-done.17 = bf16[2,64,2048]{2,1,0:T(8,128)(2,1)S(1)} collective-permute-done((bf16[2,64,2048]{2,1,0:T(8,128)(2,1)S(1)}, bf16[2,64,2048]{2,1,0:T(8,128)(2,1)S(1)}, u32[]{:S(2)}, u32[]{:S(2)}) %collective-permute-start.17) | collective-permute-done | bytes 524320 | tf_op jit(solution)/shard_map/ppermute | solution.py:710
  368.0 5.1 all-to-all-start.2
  379.7 11.2 %collective-permute-done.19.refs_5_ = bf16[2,64,2048]{2,1,0:T(8,128)(2,1)S(1)} collective-permute-done((bf16[2,64,2048]{2,1,0:T(8,128)(2,1)S(1)}, bf16[2,64,2048]{2,1,0:T(8,128)(2,1)S(1)}, u32[]{:S(2)}, u32[]{:S(2)}) %collective-permute-start.19) | collective-permute-done | bytes 524320 | tf_op jit(solution)/shard_map/ppermute | solution.py:774
  390.9 12.0 %collective-permute-done.21.refs_6_ = bf16[2,64,2048]{2,1,0:T(8,128)(2,1)S(1)} collective-permute-done((bf16[2,64,2048]{2,1,0:T(8,128)(2,1)S(1)}, bf16[2,64,2048]{2,1,0:T(8,128)(2,1)S(1)}, u32[]{:S(2)}, u32[]{:S(2)}) %collective-permute-start.21) | collective-permute-done | bytes 524320 | tf_op jit(solution)/shard_map/ppermute | solution.py:774
  405.7 5.2 all-to-all-done.2.refs_10_
  410.9 19.8 %feed_forward.1 = (bf16[2,64,2048]{2,1,0:T(8,128)(2,1)}, bf16[2,64,2048]{2,1,0:T(8,128)(2,1)}, bf16[2,64,2048]{2,1,0:T(8,128)(2,1)}, bf16[2,64,2048]{2,1,0:T(8,1...) custom-call(s32[5]{0:T(128)} %copy-done.29, ...), custom_call_target="tpu_custom_call" | custom-call | flops 8053063680 | bytes 25165824 | tf_op jit(solution)/shard_map/feed_forward/pallas_call | solution.py:668
  439.7 5.7 ffn_out.1
  445.5 4.9 convolution_convert_fusion
  450.4 10.2 %collective-permute-done.32 = bf16[2,64,2048]{2,1,0:T(8,128)(2,1)S(1)} collective-permute-done((bf16[2,64,2048]{2,1,0:T(8,128)(2,1)S(1)}, bf16[2,64,2048]{2,1,0:T(8,128)(2,1)S(1)}, u32[]{:S(2)}, u32[]{:S(2)}) %collective-permute-start.32) | collective-permute-done | bytes 524320 | tf_op jit(solution)/shard_map/ppermute | solution.py:774
  463.7 11.3 %collective-permute-done.34 = bf16[2,64,2048]{2,1,0:T(8,128)(2,1)S(1)} collective-permute-done((bf16[2,64,2048]{2,1,0:T(8,128)(2,1)S(1)}, bf16[2,64,2048]{2,1,0:T(8,128)(2,1)S(1)}, u32[]{:S(2)}, u32[]{:S(2)}) %collective-permute-start.34) | collective-permute-done | bytes 524320 | tf_op jit(solution)/shard_map/ppermute | solution.py:710
  482.0 4.8 all-to-all-start.3
  492.9 10.4 %collective-permute-done.36.refs_6_ = bf16[2,64,2048]{2,1,0:T(8,128)(2,1)} collective-permute-done((bf16[2,64,2048]{2,1,0:T(8,128)(2,1)S(1)}, bf16[2,64,2048]{2,1,0:T(8,128)(2,1)}, u32[]{:S(2)}, u32[]{:S(2)}) %collective-permute-start.36) | collective-permute-done | bytes 524320 | tf_op jit(solution)/shard_map/ppermute | solution.py:774
  510.1 14.7 %attention_backward.1 = (bf16[1024,384]{1,0:T(8,128)(2,1)S(1)}, f32[32,128]{1,0:T(8,128)S(1)}, bf16[1024,2048]{1,0:T(8,128)(2,1)S(1)}) custom-call(s32[5]{0:T(128)S(1)} %copy-done.30, bf16[2,64,2048]{2,1,0:T(8,128)(2,1)S(1)} %collective-permute-done.43.refs_0_, bf16[2,64,2048]{2,1,0:T(8,128)(2,1)S(1)} %collective-permute-done.44.refs_1_, ...), custom_call_target="tpu_custom_call" | custom-call | tf_op jit(solution)/shard_map/attention_backward/pallas_call | solution.py:256
  558.8 8.4 %collective-permute-done.51 = bf16[2,64,2048]{2,1,0:T(8,128)(2,1)} collective-permute-done((bf16[2,64,2048]{2,1,0:T(8,128)(2,1)}, bf16[2,64,2048]{2,1,0:T(8,128)(2,1)}, u32[]{:S(2)}, u32[]{:S(2)}) %collective-permute-start.51) | collective-permute-done | bytes 524320 | tf_op jit(solution)/shard_map/ppermute | solution.py:774
  569.3 6.3 owner_grads.2
  577.8 17.9 %collective-permute-done.54 = bf16[2,64,2048]{2,1,0:T(8,128)(2,1)S(1)} collective-permute-done((bf16[2,64,2048]{2,1,0:T(8,128)(2,1)S(1)}, bf16[2,64,2048]{2,1,0:T(8,128)(2,1)S(1)}, u32[]{:S(2)}, u32[]{:S(2)}) %collective-permute-start.54) | collective-permute-done | bytes 524320 | tf_op jit(solution)/shard_map/ppermute | solution.py:710
  606.7 10.9 %collective-permute-done.55 = bf16[2,64,2048]{2,1,0:T(8,128)(2,1)S(1)} collective-permute-done((bf16[2,64,2048]{2,1,0:T(8,128)(2,1)S(1)}, bf16[2,64,2048]{2,1,0:T(8,128)(2,1)S(1)}, u32[]{:S(2)}, u32[]{:S(2)}) %collective-permute-start.55) | collective-permute-done | bytes 524320 | tf_op jit(solution)/shard_map/ppermute | solution.py:774
  623.8 5.0 collective-permute-done.57
  630.7 12.8 %all-to-all-done.5.got_ref = bf16[8,448,256]{2,1,0:T(8,128)(2,1)S(1)} async-done(((bf16[8,448,256]{2,1,0:T(8,128)(2,1)}), bf16[8,448,256]{2,1,0:T(8,128)(2,1)S(1)}, u32[]{:S(2)}, u32[]{:S(2)}) %all-to-all-start.5) | async-done | bytes 1835040 | tf_op jit(solution)/shard_map/all_to_all | solution.py:706
  (338 shorter events, 167.9 us)
Async XLA Ops:
  5.8 41.5 %collective-permute-start.4 = (bf16[256,2048]{1,0:T(8,128)(2,1)}, bf16[256,2048]{1,0:T(8,128)(2,1)}, u32[]{:S(2)}, u32[]{:S(2)}) collective-permute-start(bf16[256,2048]{1,0:T(8,128)(2,1)} %param.13), channel_id=1, source_target_pairs={{0,4},{4,0},{1,5},{5,1},{2,6},{6,2},{3,7},{7,3},{8,12},{12,8},{9,1... | collective-permute-start | bytes 3145736 | tf_op jit(solution)/shard_map/ppermute | solution.py:710
  9.0 54.4 %all-to-all-start = ((bf16[8,264,512]{2,1,0:T(8,128)(2,1)}), bf16[8,264,512]{2,1,0:T(8,128)(2,1)S(1)}, u32[]{:S(2)}, u32[]{:S(2)}) async-start(bf16[8,264,512]{2,1,0:T(8,128)(2,1)} %attention_blocks.1), calls=%async_computation | async-start | bytes 4325376 | tf_op jit(solution)/shard_map/all_to_all | solution.py:706
  27.3 25.6 %collective-permute-start.5 = (bf16[2,64,2048]{2,1,0:T(8,128)(2,1)}, bf16[2,64,2048]{2,1,0:T(8,128)(2,1)S(1)}, u32[]{:S(2)}, u32[]{:S(2)}) collective-permute-start(bf16[2,64,2048]{2,1,0:T(8,128)(2,1)} %collective-permute-done), channel_id=1, source_target_pairs={{0,4},{4,0},{1,5},{5,1},{2,6},{6,2},{3,7},{7,3},{8,12},{12,8},{9,1... | collective-permute-start | bytes 1572872 | tf_op jit(solution)/shard_map/ppermute | solution.py:710
  63.5 290.0 %all-to-all-start.1 = ((bf16[8,576,256]{2,1,0:T(8,128)(2,1)}), bf16[8,576,256]{2,1,0:T(8,128)(2,1)}, u32[]{:S(2)}, u32[]{:S(2)}) async-start(bf16[8,576,256]{2,1,0:T(8,128)(2,1)} %copy-done.11), calls=%async_computation.1 | async-start | bytes 4718592 | tf_op jit(solution)/shard_map/all_to_all | solution.py:706
  89.0 262.4 %collective-permute-start.11 = (bf16[2,64,2048]{2,1,0:T(8,128)(2,1)}, bf16[2,64,2048]{2,1,0:T(8,128)(2,1)}, u32[]{:S(2)}, u32[]{:S(2)}) collective-permute-start(bf16[2,64,2048]{2,1,0:T(8,128)(2,1)} %add_convert_fusion.6), channel_id=1, source_target_pairs={{0,3},{1,2},{2,1},{3,0},{4,7},{5,6},{6,5},{7,4},{8,11},{9,10},{10,... | collective-permute-start | bytes 1572872 | tf_op jit(solution)/shard_map/ppermute | solution.py:774
  92.4 259.1 %collective-permute-start.14 = (bf16[2,64,2048]{2,1,0:T(8,128)(2,1)}, bf16[2,64,2048]{2,1,0:T(8,128)(2,1)}, u32[]{:S(2)}, u32[]{:S(2)}) collective-permute-start(bf16[2,64,2048]{2,1,0:T(8,128)(2,1)} %add_convert_fusion.5), channel_id=1, source_target_pairs={{0,2},{1,3},{2,0},{3,1},{4,6},{5,7},{6,4},{7,5},{8,10},{9,11},{10,... | collective-permute-start | bytes 1572872 | tf_op jit(solution)/shard_map/ppermute | solution.py:774
  93.8 257.6 %collective-permute-start.16 = (bf16[2,64,2048]{2,1,0:T(8,128)(2,1)}, bf16[2,64,2048]{2,1,0:T(8,128)(2,1)}, u32[]{:S(2)}, u32[]{:S(2)}) collective-permute-start(bf16[2,64,2048]{2,1,0:T(8,128)(2,1)} %add_convert_fusion.4), channel_id=1, source_target_pairs={{0,1},{1,0},{2,3},{3,2},{4,5},{5,4},{6,7},{7,6},{8,9},{9,8},{10,11... | collective-permute-start | bytes 1572872 | tf_op jit(solution)/shard_map/ppermute | solution.py:774
  94.3 257.1 %collective-permute-start.9 = (bf16[2,64,2048]{2,1,0:T(8,128)(2,1)}, bf16[2,64,2048]{2,1,0:T(8,128)(2,1)}, u32[]{:S(2)}, u32[]{:S(2)}) collective-permute-start(bf16[2,64,2048]{2,1,0:T(8,128)(2,1)} %get-tuple-element.110), channel_id=1, source_target_pairs={{0,4},{4,0},{1,5},{5,1},{2,6},{6,2},{3,7},{7,3},{8,12},{12,8},{9,1... | collective-permute-start | bytes 1572872 | tf_op jit(solution)/shard_map/ppermute | solution.py:710
  368.0 42.9 %all-to-all-start.2 = ((bf16[8,256,384]{2,1,0:T(8,128)(2,1)}), bf16[8,256,384]{2,1,0:T(8,128)(2,1)}, u32[]{:S(2)}, u32[]{:S(2)}) async-start(bf16[8,256,384]{2,1,0:T(8,128)(2,1)} %copy-done.15), calls=%async_computation.2 | async-start | bytes 3145728 | tf_op jit(solution)/shard_map/all_to_all | solution.py:706
  377.7 25.3 %collective-permute-start.21 = (bf16[2,64,2048]{2,1,0:T(8,128)(2,1)S(1)}, bf16[2,64,2048]{2,1,0:T(8,128)(2,1)S(1)}, u32[]{:S(2)}, u32[]{:S(2)}) collective-permute-start(bf16[2,64,2048]{2,1,0:T(8,128)(2,1)S(1)} %multiply_convert_fusion.1.refs_4_), channel_id=1, source_target_pairs={{0,2},{1,3},{2,0},{3,1},{4,6},{5,7},{6,4},{7,5},{8,10},{9,11},{10,... | collective-permute-start | bytes 1572872 | tf_op jit(solution)/shard_map/ppermute | solution.py:774
  379.2 23.8 %collective-permute-start.23 = (bf16[2,64,2048]{2,1,0:T(8,128)(2,1)S(1)}, bf16[2,64,2048]{2,1,0:T(8,128)(2,1)S(1)}, u32[]{:S(2)}, u32[]{:S(2)}) collective-permute-start(bf16[2,64,2048]{2,1,0:T(8,128)(2,1)S(1)} %multiply_convert_fusion.1.refs_4_), channel_id=1, source_target_pairs={{0,3},{1,2},{2,1},{3,0},{4,7},{5,6},{6,5},{7,4},{8,11},{9,10},{10,... | collective-permute-start | bytes 1572872 | tf_op jit(solution)/shard_map/ppermute | solution.py:774
  379.7 23.8 %collective-permute-start.18 = (bf16[2,64,2048]{2,1,0:T(8,128)(2,1)S(1)}, bf16[2,64,2048]{2,1,0:T(8,128)(2,1)S(1)}, u32[]{:S(2)}, u32[]{:S(2)}) collective-permute-start(bf16[2,64,2048]{2,1,0:T(8,128)(2,1)S(1)} %multiply_convert_fusion.1.refs_4_), channel_id=1, source_target_pairs={{0,4},{4,0},{1,5},{5,1},{2,6},{6,2},{3,7},{7,3},{8,12},{12,8},{9,1... | collective-permute-start | bytes 1572872 | tf_op jit(solution)/shard_map/ppermute | solution.py:710
  463.1 23.7 %collective-permute-start.30 = (bf16[2,64,2048]{2,1,0:T(8,128)(2,1)}, bf16[2,64,2048]{2,1,0:T(8,128)(2,1)}, u32[]{:S(2)}, u32[]{:S(2)}) collective-permute-start(bf16[2,64,2048]{2,1,0:T(8,128)(2,1)} %get-tuple-element.141), channel_id=1, source_target_pairs={{0,4},{4,0},{1,5},{5,1},{2,6},{6,2},{3,7},{7,3},{8,12},{12,8},{9,1... | collective-permute-start | bytes 1572872 | tf_op jit(solution)/shard_map/ppermute | solution.py:710
  463.2 25.7 %collective-permute-start.39 = (bf16[2,64,2048]{2,1,0:T(8,128)(2,1)}, bf16[2,64,2048]{2,1,0:T(8,128)(2,1)}, u32[]{:S(2)}, u32[]{:S(2)}) collective-permute-start(bf16[2,64,2048]{2,1,0:T(8,128)(2,1)} %get-tuple-element.148), channel_id=1, source_target_pairs={{0,4},{4,0},{1,5},{5,1},{2,6},{6,2},{3,7},{7,3},{8,12},{12,8},{9,1... | collective-permute-start | bytes 1572872 | tf_op jit(solution)/shard_map/ppermute | solution.py:710
  479.4 23.9 %collective-permute-start.36 = (bf16[2,64,2048]{2,1,0:T(8,128)(2,1)S(1)}, bf16[2,64,2048]{2,1,0:T(8,128)(2,1)}, u32[]{:S(2)}, u32[]{:S(2)}) collective-permute-start(bf16[2,64,2048]{2,1,0:T(8,128)(2,1)S(1)} %get-tuple-element.188.refs_4_), channel_id=1, source_target_pairs={{0,2},{1,3},{2,0},{3,1},{4,6},{5,7},{6,4},{7,5},{8,10},{9,11},{10,... | collective-permute-start | bytes 1572872 | tf_op jit(solution)/shard_map/ppermute | solution.py:774
  482.0 65.1 %all-to-all-start.3 = ((bf16[8,256,640]{2,1,0:T(8,128)(2,1)}), bf16[8,256,640]{2,1,0:T(8,128)(2,1)}, u32[]{:S(2)}, u32[]{:S(2)}) async-start(bf16[8,256,640]{2,1,0:T(8,128)(2,1)} %bitcast.81), calls=%async_computation.3 | async-start | bytes 5242880 | tf_op jit(solution)/shard_map/all_to_all | solution.py:706
  505.2 33.0 %collective-permute-start.29 = (bf16[2,64,2048]{2,1,0:T(8,128)(2,1)}, bf16[2,64,2048]{2,1,0:T(8,128)(2,1)S(1)}, u32[]{:S(2)}, u32[]{:S(2)}) collective-permute-start(bf16[2,64,2048]{2,1,0:T(8,128)(2,1)} %copy-done.33), channel_id=1, source_target_pairs={{0,4},{4,0},{1,5},{5,1},{2,6},{6,2},{3,7},{7,3},{8,12},{12,8},{9,1... | collective-permute-start | bytes 1572872 | tf_op jit(solution)/shard_map/ppermute | solution.py:710
  508.1 24.8 %collective-permute-start.40 = (bf16[2,64,2048]{2,1,0:T(8,128)(2,1)S(1)}, bf16[2,64,2048]{2,1,0:T(8,128)(2,1)S(1)}, u32[]{:S(2)}, u32[]{:S(2)}) collective-permute-start(bf16[2,64,2048]{2,1,0:T(8,128)(2,1)S(1)} %convert_add_fusion.4), channel_id=1, source_target_pairs={{0,2},{1,3},{2,0},{3,1},{4,6},{5,7},{6,4},{7,5},{8,10},{9,11},{10,... | collective-permute-start | bytes 1572872 | tf_op jit(solution)/shard_map/ppermute | solution.py:774
  509.4 23.9 %collective-permute-start.42 = (bf16[2,64,2048]{2,1,0:T(8,128)(2,1)S(1)}, bf16[2,64,2048]{2,1,0:T(8,128)(2,1)S(1)}, u32[]{:S(2)}, u32[]{:S(2)}) collective-permute-start(bf16[2,64,2048]{2,1,0:T(8,128)(2,1)S(1)} %convert_add_fusion.3), channel_id=1, source_target_pairs={{0,1},{1,0},{2,3},{3,2},{4,5},{5,4},{6,7},{7,6},{8,9},{9,8},{10,11... | collective-permute-start | bytes 1572872 | tf_op jit(solution)/shard_map/ppermute | solution.py:774
  543.1 24.1 %collective-permute-start.51 = (bf16[2,64,2048]{2,1,0:T(8,128)(2,1)}, bf16[2,64,2048]{2,1,0:T(8,128)(2,1)}, u32[]{:S(2)}, u32[]{:S(2)}) collective-permute-start(bf16[2,64,2048]{2,1,0:T(8,128)(2,1)} %add_convert_fusion.1), channel_id=1, source_target_pairs={{0,2},{1,3},{2,0},{3,1},{4,6},{5,7},{6,4},{7,5},{8,10},{9,11},{10,... | collective-permute-start | bytes 1572872 | tf_op jit(solution)/shard_map/ppermute | solution.py:774
  544.8 22.5 %collective-permute-start.53 = (bf16[2,64,2048]{2,1,0:T(8,128)(2,1)}, bf16[2,64,2048]{2,1,0:T(8,128)(2,1)}, u32[]{:S(2)}, u32[]{:S(2)}) collective-permute-start(bf16[2,64,2048]{2,1,0:T(8,128)(2,1)} %add_convert_fusion), channel_id=1, source_target_pairs={{0,1},{1,0},{2,3},{3,2},{4,5},{5,4},{6,7},{7,6},{8,9},{9,8},{10,11... | collective-permute-start | bytes 1572872 | tf_op jit(solution)/shard_map/ppermute | solution.py:774
  547.1 49.4 %all-to-all-start.4 = ((bf16[8,264,384]{2,1,0:T(8,128)(2,1)}), bf16[8,264,384]{2,1,0:T(8,128)(2,1)S(1)}, u32[]{:S(2)}, u32[]{:S(2)}) async-start(bf16[8,264,384]{2,1,0:T(8,128)(2,1)} %fusion.6), calls=%async_computation.4 | async-start | bytes 3244032 | tf_op jit(solution)/shard_map/all_to_all | solution.py:706
  596.5 47.0 %all-to-all-start.5 = ((bf16[8,448,256]{2,1,0:T(8,128)(2,1)}), bf16[8,448,256]{2,1,0:T(8,128)(2,1)S(1)}, u32[]{:S(2)}, u32[]{:S(2)}) async-start(bf16[8,448,256]{2,1,0:T(8,128)(2,1)} %pad_maximum_fusion), calls=%async_computation.5 | async-start | bytes 3670016 | tf_op jit(solution)/shard_map/all_to_all | solution.py:706
  604.9 23.9 %collective-permute-start.57 = (bf16[2,64,2048]{2,1,0:T(8,128)(2,1)S(1)}, bf16[2,64,2048]{2,1,0:T(8,128)(2,1)S(1)}, u32[]{:S(2)}, u32[]{:S(2)}) collective-permute-start(bf16[2,64,2048]{2,1,0:T(8,128)(2,1)S(1)} %pad_maximum_fusion.3), channel_id=1, source_target_pairs={{0,3},{1,2},{2,1},{3,0},{4,7},{5,6},{6,5},{7,4},{8,11},{9,10},{10,... | collective-permute-start | bytes 1572872 | tf_op jit(solution)/shard_map/ppermute | solution.py:774
  (108 other events, 1426.1 us)
